TPU v7x, 128 devices: a whole 4x4x4 slice. The times are simulated.
128 devices in a mesh: dom: 128 (over y, z, x, core).
Axes of the slice: x: 4, y: 4, z: 4, core: 2. Of those that a mesh axis runs over, the one named last changes fastest.
Arguments:
- right_side: float32 [8, 2097152], P(None, 'dom'), may hold values from -24 to 24, as said below
- stiffness: float32 [3, 125, 32768], P(None, None, 'dom'), may hold values from 0.005 to 0.05
- mass: float32 [125, 32768], P(None, 'dom'), may hold values from 0.5 to 2
- region: int32 [32768], P('dom'), may hold values from 0 to 2
- density: float32 [3], replicated, may hold values from 0.5 to 2
- elem_nodes: int32 [125, 32768], P(None, 'dom'), may hold values from 0 to 32767, as said below
- peer_rank: int32 [128, 5], P('dom'), may hold values from 0 to 127, as said below
- send_nodes: int32 [128, 5, 128], P('dom'), may hold values from 0 to 16383, as said below
Outputs:
- solution: float32 [8, 2097152], P(None, 'dom')
- residual: float32 [8, 2097152], P(None, 'dom')
Inputs may be any that keep to these rules, and one draw needn't show every extreme that they name: `right_side`: A mean scale that rises along the partitions. `peer_rank`: the peers of partition r, in a drawn order: r + 1 and r - 1 modulo 128, and r XOR 2**k for 3 bit positions k between 1 and log2(128) - 1 that are the same for every partition, the highest one among them. Peers are mutual. `send_nodes`: repeats are possible within one list. `elem_nodes`: A value 16384 + s * 128 + c names slot c of what peer s shares with this partition. Elements 2 g and 2 g + 1 of a partition name own nodes only from 128 g to 128 g + 127, each of them at least once. List the received slots of a partition in the order of its peer_rank slots, slot c fastest, and repeat that list cyclically: for g < 64 the elements 2 g and 2 g + 1 also name exactly the entries g * 10 to (g + 1) * 10 - 1 of it, each once; other elements name no received slot.
All inputs are finite; a program needn't handle non-finite values.
Results may differ from a plain program's by a relative error of at most 0.0003.
Values sent between devices are 32-bit elements; how exact they have to be, the bound alone decides.
A program may use at most 128 MiB of HBM per device.

v0:
```python
import jax
import jax.numpy as jnp
import numpy as np
from jax import lax
from jax.sharding import PartitionSpec as P

NPE = 125
ITERS = 2


precise = lax.Precision.HIGHEST


def gll_matrix():
    points = np.array([-1.0, -np.sqrt(3.0 / 7.0), 0.0, np.sqrt(3.0 / 7.0), 1.0])
    weights = np.array(
        [
            1.0 / np.prod([points[column] - points[other] for other in range(5) if other != column])
            for column in range(5)
        ]
    )
    matrix = np.zeros((5, 5))
    for row_index in range(5):
        for column in range(5):
            if row_index != column:
                matrix[row_index, column] = (
                    weights[column] / weights[row_index] / (points[row_index] - points[column])
                )
        matrix[row_index, row_index] = -np.sum(matrix[row_index])
    return matrix


def element_apply(gathered, stiff_grid, mass_grid, derivative):
    grad_first = jnp.einsum("ai,vijke->vajke", derivative, gathered, precision=precise)
    result = jnp.einsum(
        "ai,vajke->vijke", derivative, stiff_grid[0] * grad_first, precision=precise
    )
    grad_second = jnp.einsum("bj,vijke->vibke", derivative, gathered, precision=precise)
    result = result + jnp.einsum(
        "bj,vibke->vijke", derivative, stiff_grid[1] * grad_second, precision=precise
    )
    grad_third = jnp.einsum("ck,vijke->vijce", derivative, gathered, precision=precise)
    result = result + jnp.einsum(
        "ck,vijce->vijke", derivative, stiff_grid[2] * grad_third, precision=precise
    )
    return result + mass_grid * gathered


def element_diagonal(stiff_grid, mass_grid, derivative):
    square = derivative * derivative
    first = jnp.einsum("ai,ajke->ijke", square, stiff_grid[0], precision=precise)
    second = jnp.einsum("bj,ibke->ijke", square, stiff_grid[1], precision=precise)
    third = jnp.einsum("ck,ijce->ijke", square, stiff_grid[2], precision=precise)
    return first + second + third + mass_grid


def on_device(right_side, stiffness, mass, region, density, elem_nodes, peer_rank, send_nodes):
    derivative = jnp.asarray(gll_matrix(), jnp.float32)
    vectors, own_count = right_side.shape
    elem_count = elem_nodes.shape[1]
    edge_count = elem_count // 2
    pair_count = elem_count // 2
    edge_pairs = edge_count // 2
    window = own_count // pair_count
    devices = lax.axis_size("dom")
    peer_count = peer_rank.shape[1]
    slot_count = send_nodes.shape[2]
    live = peer_count * slot_count
    run_length = (live + edge_pairs - 1) // edge_pairs
    send_flat = send_nodes[0].reshape(-1)
    peer_row = peer_rank[0]
    routing = (jnp.arange(devices, dtype=jnp.int32)[:, None] == peer_row[None, :]).astype(
        jnp.float32
    )
    region_hot = (region[None, :] == jnp.arange(3, dtype=jnp.int32)[:, None]).astype(jnp.float32)
    mass_grid = (jnp.sum(region_hot * density[:, None], axis=0)[None, :] * mass).reshape(
        5, 5, 5, elem_count
    )
    stiff_grid = stiffness.reshape(3, 5, 5, 5, elem_count)
    pairs = elem_nodes.reshape(NPE, pair_count, 2)
    window_base = (jnp.arange(pair_count, dtype=jnp.int32) * window)[None, :, None]
    own_hot = ((pairs - window_base)[..., None] == jnp.arange(window, dtype=jnp.int32)).astype(
        jnp.float32
    )
    edge_refs = pairs[:, :edge_pairs] - own_count
    is_ghost = edge_refs >= 0
    sender = jnp.where(is_ghost, edge_refs // slot_count, -1)
    column = jnp.where(is_ghost, edge_refs % slot_count, 0)
    slot_of = jnp.sum(
        jnp.arange(peer_count, dtype=jnp.int32) * (sender[..., None] == peer_row).astype(jnp.int32),
        axis=-1,
    )
    compact = slot_of * slot_count + column
    run_base = (jnp.arange(edge_pairs, dtype=jnp.int32) * run_length)[None, :, None]
    offset = (compact - run_base) % live
    ghost_hot = (
        is_ghost[..., None] & (offset[..., None] == jnp.arange(run_length, dtype=jnp.int32))
    ).astype(jnp.float32)
    fold = (
        jnp.arange(edge_pairs * run_length, dtype=jnp.int32)[:, None] % live
        == jnp.arange(live, dtype=jnp.int32)[None, :]
    ).astype(jnp.float32)

    def scatter_own(values):
        rows = values.shape[0]
        summed = jnp.einsum(
            "ngew,vnge->vgw", own_hot, values.reshape(rows, NPE, pair_count, 2), precision=precise
        )
        return summed.reshape(rows, own_count)

    def return_sums(edge_values):
        rows = edge_values.shape[0]
        run_sums = jnp.einsum(
            "ngeh,vnge->vgh",
            ghost_hot,
            edge_values.reshape(rows, NPE, edge_pairs, 2),
            precision=precise,
        )
        slots = jnp.einsum(
            "vj,jk->vk", run_sums.reshape(rows, -1), fold, precision=precise
        ).reshape(rows, peer_count, slot_count)
        pending = jnp.einsum("vpc,np->vnc", slots, routing, precision=precise)
        returned = lax.all_to_all(pending, "dom", split_axis=1, concat_axis=1, tiled=True)
        return jnp.einsum("vnc,np->vpc", returned, routing, precision=precise).reshape(rows, -1)

    diag_terms = element_diagonal(stiff_grid, mass_grid, derivative).reshape(1, NPE, elem_count)
    diagonal = (
        scatter_own(diag_terms).at[:, send_flat].add(return_sums(diag_terms[:, :, :edge_count]))
    )

    def norm_sum(residual, precond):
        return lax.psum(jnp.sum(residual * precond, axis=1), "dom")

    solution = jnp.zeros_like(right_side)
    residual = right_side
    precond = residual / diagonal
    direction = precond
    product_now = norm_sum(residual, precond)
    for iteration in range(ITERS):
        send_picked = jnp.take(direction, send_flat, axis=1).reshape(vectors, -1, slot_count)
        outgoing = jnp.einsum("vpc,np->vnc", send_picked, routing, precision=precise)
        incoming = lax.all_to_all(outgoing, "dom", split_axis=1, concat_axis=1, tiled=True)
        send_slots = jnp.einsum("vnc,np->vpc", incoming, routing, precision=precise).reshape(
            vectors, live
        )
        send_runs = jnp.einsum("vk,jk->vj", send_slots, fold, precision=precise)
        operator_runs = send_runs.reshape(vectors, edge_pairs, run_length)
        gather_rows = direction.shape[0]
        gather_picked = jnp.einsum(
            "ngew,vgw->vnge",
            own_hot,
            direction.reshape(gather_rows, pair_count, window),
            precision=precise,
        )
        own_values = gather_picked.reshape(gather_rows, NPE, elem_count)
        picked = jnp.einsum("ngeh,vgh->vnge", ghost_hot, operator_runs, precision=precise)
        operator_edge_values = own_values[:, :, :edge_count] + picked.reshape(
            vectors, NPE, edge_count
        )
        gathered = jnp.concatenate([operator_edge_values, own_values[:, :, edge_count:]], axis=2)
        block_width = elem_count - 0
        grid = gathered.reshape(vectors, 5, 5, 5, block_width)
        result = element_apply(grid, stiff_grid, mass_grid, derivative)
        operator_result = result.reshape(vectors, NPE, block_width)
        owned_rows = scatter_own(operator_result)
        applied = owned_rows.at[:, send_flat].add(return_sums(operator_result[:, :, :edge_count]))
        step_size = product_now / lax.psum(jnp.sum(direction * applied, axis=1), "dom")
        solution = solution + step_size[:, None] * direction
        residual = residual - step_size[:, None] * applied
        if iteration + 1 < ITERS:
            precond = residual / diagonal
            product_next = norm_sum(residual, precond)
            direction = precond + (product_next / product_now)[:, None] * direction
            product_now = product_next
    return (solution, residual)


def solution(mesh):
    placed = (
        P(None, "dom"),
        P(None, None, "dom"),
        P(None, "dom"),
        P("dom"),
        P(),
        P(None, "dom"),
        P("dom", None),
        P("dom", None, None),
    )
    return jax.shard_map(
        on_device,
        mesh=mesh,
        in_specs=placed,
        out_specs=(P(None, "dom"), P(None, "dom")),
        check_vma=False,
    )
```

profile of v0, /device:TPU:1, one launch (start us, length us, event | category | flops | bytes accessed | tf_op | source)
XLA Modules:
  0.0 541.5 jit_solution(16329869097775111692)
XLA Ops:
  11.3 11.5 %all-to-all-start = ((f32[1,128,128]{2,0,1:T(1,128)}), f32[1,128,128]{2,0,1:T(1,128)S(1)}, u32[]{:S(2)}, u32[]{:S(2)}) async-start(f32[1,128,128]{2,0,1:T(1,128)} %bitcast.21), calls=%async_computation | async-start | bytes 131072 | tf_op jit(solution)/shard_map/all_to_all | solution.py:123
  25.6 3.1 copy.153
  29.0 3.7 reshape.364
  32.7 5.2 copy.162
  37.9 9.6 %fusion.4 = f32[128,1,128,1]{2,1,3,0:T(1,128)S(1)} fusion(f32[125,128,2,1]{0,3,2,1:T(1,128)S(1)} %bitcast.270, s32[125,128,2]{0,2,1:T(2,128)S(1)} %broadcast_subtract_fusion), kind=kOutput, calls=%fused_computation.12 | convolution fusion | flops 53248000 | bytes 321536 | tf_op jit(solution)/shard_map/ngew,vnge->vgw/dot_general | solution.py:106
  47.7 4.7 scatter_fusion
  52.4 7.9 %broadcast_divide_fusion = f32[8,16384]{0,1:T(8,128)} fusion(f32[8,16384]{0,1:T(8,128)} %copy.162, f32[16384]{0:T(1024)S(1)} %scatter_fusion), kind=kLoop, calls=%fused_computation.26 | loop fusion | flops 131072 | bytes 1114112 | tf_op jit(solution)/shard_map/div | solution.py:136
  60.4 5.0 gather_fusion
  67.3 9.8 %all-to-all-start.1 = ((f32[8,128,128]{2,0,1:T(8,128)}), f32[8,128,128]{2,0,1:T(8,128)S(1)}, u32[]{:S(2)}, u32[]{:S(2)}) async-start(f32[8,128,128]{2,0,1:T(8,128)} %copy.167), calls=%async_computation.1 | async-start | bytes 1048576 | tf_op jit(solution)/shard_map/all_to_all | solution.py:142
  77.1 15.3 %fusion.3 = f32[128,8,125,2]{2,1,3,0:T(8,128)S(1)} fusion(f32[8,128,128,1]{0,2,3,1:T(8,128)} %bitcast.253, s32[125,128,2]{0,2,1:T(2,128)S(1)} %broadcast_subtract_fusion), kind=kOutput, calls=%fused_computation.11 | convolution fusion | flops 397312000 | bytes 1676288 | tf_op jit(solution)/shard_map/ngew,vgw->vnge/dot_general | solution.py:149
  93.4 2.0 fusion.37
  96.7 1.8 fusion.26
  98.5 1.8 fusion.28
  100.3 1.8 fusion.12
  102.2 1.6 fusion.19
  103.8 1.6 fusion.20
  105.4 3.1 fusion.14
  108.9 9.2 %copy.183 = f32[8,5,5,5,256]{0,4,3,2,1:T(8,128)} copy(f32[8,5,5,5,256]{4,1,3,2,0:T(8,128)S(1)} %fusion.14) | data formatting | bytes 2048000 | tf_op jit(solution)/shard_map/add | solution.py:46
  118.4 1.5 convolution_bitcast_fusion.7
  122.6 9.8 %all-to-all-start.2 = ((f32[8,128,128]{2,0,1:T(8,128)}), f32[8,128,128]{2,0,1:T(8,128)S(1)}, u32[]{:S(2)}, u32[]{:S(2)}) async-start(f32[8,128,128]{2,0,1:T(8,128)} %copy.189), calls=%async_computation.2 | async-start | bytes 1048576 | tf_op jit(solution)/shard_map/all_to_all | solution.py:123
  132.3 21.9 %convolution_bitcast_fusion.1 = f32[8,16384]{1,0:T(8,128)S(1)} fusion(f32[8,125,128,2]{0,3,2,1:T(2,128)} %bitcast.244, s32[125,128,2]{0,2,1:T(2,128)S(1)} %broadcast_subtract_fusion), kind=kOutput, calls=%fused_computation.6 | convolution fusion | flops 397312000 | bytes 1676288 | tf_op jit(solution)/shard_map/ngew,vnge->vgw/dot_general | solution.py:106
  154.2 5.3 copy.191
  160.0 12.0 %scatter_fusion.1 = f32[8,16384]{0,1:T(8,128)} fusion(f32[8,16384]{0,1:T(8,128)} %copy.191, s32[640]{0:T(1024)S(1)} %fusion.96, f32[640,8]{1,0:T(8,128)S(1)} %copy.192), kind=kCustom, calls=%fused_computation.3 | custom fusion | flops 5120 | bytes 64000 | tf_op jit(solution)/shard_map/scatter-add | solution.py:166
  172.0 7.3 %multiply_reduce_fusion.2 = (f32[8]{0:T(128)S(1)}, f32[8]{0:T(128)S(1)}) fusion(f32[8,16384]{0,1:T(8,128)} %scatter_fusion.1, f32[8,16384]{0,1:T(8,128)} %copy.162, f32[16384]{0:T(1024)S(1)} %scatter_fusion), kind=kLoop, calls=%fused_computation.19 | loop fusion | flops 655344 | bytes 1114176 | tf_op jit(solution)/shard_map/reduce_sum | solution.py:167
  179.4 67.2 %all-reduce = (f32[8]{0:T(128)S(1)}, f32[8]{0:T(128)S(1)}) all-reduce(f32[8]{0:T(128)S(1)} %get-tuple-element.12, f32[8]{0:T(128)S(1)} %get-tuple-element.11), channel_id=1, replica_groups=mesh['dom'=128] {'dom'}, use_global_device_ids=true, to_apply=%region_4.5 | all-reduce | flops 16 | bytes 128 | tf_op jit(solution)/shard_map/psum | solution.py:132
  246.6 9.6 %multiply_reduce_fusion.1 = (f32[8]{0:T(128)S(1)}, f32[8,16384]{0,1:T(8,128)}) fusion(f32[16384]{0:T(1024)S(1)} %scatter_fusion, f32[8,16384]{0,1:T(8,128)} %copy.162, f32[8,16384]{0,1:T(8,128)} %scatter_fusion.1, f32[8]{0:T(128)S(1)} %div.44), kind=kLoop, calls=%fused_computation.17 | loop fusion | flops 655352 | bytes 1638464 | tf_op jit(solution)/shard_map/reduce_sum | solution.py:132
  256.2 62.6 %psum.30 = f32[8]{0:T(128)S(1)} all-reduce(f32[8]{0:T(128)S(1)} %get-tuple-element.15), channel_id=1, replica_groups=mesh['dom'=128] {'dom'}, use_global_device_ids=true, to_apply=%region_9.11 | all-reduce | flops 8 | bytes 64 | tf_op jit(solution)/shard_map/psum | solution.py:132
  318.8 9.7 %multiply_add_fusion.1 = f32[8,16384]{0,1:T(8,128)} fusion(f32[8,16384]{0,1:T(8,128)} %get-tuple-element.16, f32[16384]{0:T(1024)S(1)} %scatter_fusion, f32[8]{0:T(128)S(1)} %div.46, f32[8,16384]{0,1:T(8,128)} %copy.162), kind=kLoop, calls=%fused_computation.16 | loop fusion | flops 524288 | bytes 1638432 | tf_op jit(solution)/shard_map/add | solution.py:173
  328.5 5.0 gather_fusion.1
  335.5 5.4 %all-to-all-start.3 = ((f32[8,128,128]{2,0,1:T(8,128)}), f32[8,128,128]{2,0,1:T(8,128)S(1)}, u32[]{:S(2)}, u32[]{:S(2)}) async-start(f32[8,128,128]{2,0,1:T(8,128)} %copy.197), calls=%async_computation.3 | async-start | bytes 1048576 | tf_op jit(solution)/shard_map/all_to_all | solution.py:142
  340.9 15.3 %fusion.2 = f32[128,8,125,2]{2,1,3,0:T(8,128)S(1)} fusion(f32[8,128,128,1]{0,2,3,1:T(8,128)} %bitcast.242, s32[125,128,2]{0,2,1:T(2,128)S(1)} %broadcast_subtract_fusion), kind=kOutput, calls=%fused_computation.10 | convolution fusion | flops 397312000 | bytes 1676288 | tf_op jit(solution)/shard_map/ngew,vgw->vnge/dot_general | solution.py:149
  357.2 2.0 fusion.40
  360.5 1.8 fusion.22
  362.3 1.8 fusion.24
  364.1 1.8 fusion.10
  366.0 1.6 fusion.16
  367.6 1.6 fusion.17
  369.2 2.9 fusion.15
  372.5 9.2 %copy.211 = f32[8,5,5,5,256]{0,4,3,2,1:T(8,128)} copy(f32[8,5,5,5,256]{4,1,3,2,0:T(8,128)S(1)} %fusion.15) | data formatting | bytes 2048000 | tf_op jit(solution)/shard_map/add | solution.py:46
  385.4 9.8 %all-to-all-start.4 = ((f32[8,128,128]{2,0,1:T(8,128)}), f32[8,128,128]{2,0,1:T(8,128)S(1)}, u32[]{:S(2)}, u32[]{:S(2)}) async-start(f32[8,128,128]{2,0,1:T(8,128)} %copy.217), calls=%async_computation.4 | async-start | bytes 1048576 | tf_op jit(solution)/shard_map/all_to_all | solution.py:123
  395.2 21.9 %convolution_bitcast_fusion = f32[8,16384]{1,0:T(8,128)S(1)} fusion(f32[8,125,128,2]{0,3,2,1:T(2,128)} %bitcast.243, s32[125,128,2]{0,2,1:T(2,128)S(1)} %broadcast_subtract_fusion), kind=kOutput, calls=%fused_computation.5 | convolution fusion | flops 397312000 | bytes 1676288 | tf_op jit(solution)/shard_map/ngew,vnge->vgw/dot_general | solution.py:106
  417.1 5.3 copy.219
  422.8 12.0 %scatter_fusion.2 = f32[8,16384]{0,1:T(8,128)} fusion(f32[8,16384]{0,1:T(8,128)} %copy.219, s32[640]{0:T(1024)S(1)} %fusion.96, f32[640,8]{1,0:T(8,128)S(1)} %copy.220), kind=kCustom, calls=%fused_computation.4 | custom fusion | flops 5120 | bytes 64000 | tf_op jit(solution)/shard_map/scatter-add | solution.py:166
  434.9 7.2 %multiply_reduce_fusion = f32[8]{0:T(128)S(1)} fusion(f32[8,16384]{0,1:T(8,128)} %multiply_add_fusion.1, f32[8,16384]{0,1:T(8,128)} %scatter_fusion.2), kind=kLoop, calls=%fused_computation.15 | loop fusion | flops 262136 | bytes 1048608 | tf_op jit(solution)/shard_map/reduce_sum | solution.py:167
  442.1 67.2 %psum.31 = f32[8]{0:T(128)S(1)} all-reduce(f32[8]{0:T(128)S(1)} %multiply_reduce_fusion), channel_id=1, replica_groups=mesh['dom'=128] {'dom'}, use_global_device_ids=true, to_apply=%region_12.14 | all-reduce | flops 8 | bytes 64 | tf_op jit(solution)/shard_map/psum | solution.py:167
  509.3 20.0 %multiply_subtract_fusion = (f32[8,16384]{0,1:T(8,128)}, f32[8,16384]{0,1:T(8,128)}) fusion(f32[8,16384]{0,1:T(8,128)} %get-tuple-element.16, f32[8,16384]{0,1:T(8,128)} %scatter_fusion.2, f32[8]{0:T(128)S(1)} %div.47, f32[8,16384]{0,1:T(8,128)} %multiply_add_fusion.1, f32[8,16384]{0,1:T(8,128)} %copy.162, f32[16384]{0:T(1024)S(1)} %scatter_fusion, ...), kind=kLoop, calls=%fused_computation.13 | loop fusion | flops 786432 | bytes 3211328 | tf_op jit(solution)/shard_map/sub | solution.py:169
  529.3 5.9 %copy.222 = f32[8,16384]{1,0:T(8,128)} copy(f32[8,16384]{0,1:T(8,128)} %get-tuple-element.24) | data formatting | bytes 1048576
  535.2 5.9 %copy.221 = f32[8,16384]{1,0:T(8,128)} copy(f32[8,16384]{0,1:T(8,128)} %get-tuple-element.25) | data formatting | bytes 1048576
  (140 shorter events, 30.1 us)
Async XLA Ops:
  0.6 7.1 %copy-start.12 = (f32[5,5,1,1]{0,1,3,2:T(8,128)S(1)}, f32[5,5,1,1]{0,1,3,2:T(8,128)}, u32[]{:S(2)}) copy-start(f32[5,5,1,1]{0,1,3,2:T(8,128)} %constant.78) | copy-start | bytes 304
  0.6 9.6 %copy-start.11 = (s32[1,5]{1,0:T(1,128)S(1)}, s32[1,5]{1,0:T(1,128)}, u32[]{:S(2)}) copy-start(s32[1,5]{1,0:T(1,128)} %param.17) | copy-start | bytes 64
  0.7 22.1 %copy-start.13 = (s32[1,5,128]{2,0,1:T(1,128)S(1)}, s32[1,5,128]{2,0,1:T(1,128)}, u32[]{:S(2)}) copy-start(s32[1,5,128]{2,0,1:T(1,128)} %param.18) | copy-start | bytes 7684
  3.6 92.1 %copy-start.6 = (pred[125,64,2]{0,2,1:T(4,128)(4,1)}, pred[125,64,2]{0,2,1:T(4,128)(4,1)S(1)}, u32[]{:S(2)}) copy-start(pred[125,64,2]{0,2,1:T(4,128)(4,1)S(1)} %copy.158) | copy-start | bytes 48004
  11.3 36.3 %all-to-all-start = ((f32[1,128,128]{2,0,1:T(1,128)}), f32[1,128,128]{2,0,1:T(1,128)S(1)}, u32[]{:S(2)}, u32[]{:S(2)}) async-start(f32[1,128,128]{2,0,1:T(1,128)} %bitcast.21), calls=%async_computation | async-start | bytes 131072 | tf_op jit(solution)/shard_map/all_to_all | solution.py:123
  22.8 42.6 %copy-start.14 = (pred[640]{0:T(1024)(128)(4,1)}, pred[640]{0:T(1024)(128)(4,1)S(1)}, u32[]{:S(2)}) copy-start(pred[640]{0:T(1024)(128)(4,1)S(1)} %compare_and_fusion) | copy-start | bytes 1924
  25.6 7.0 %copy-start.10 = (f32[8,16384]{1,0:T(8,128)S(1)}, f32[8,16384]{1,0:T(8,128)}, u32[]{:S(2)}) copy-start(f32[8,16384]{1,0:T(8,128)} %param.11) | copy-start | bytes 1572868
  67.3 25.7 %all-to-all-start.1 = ((f32[8,128,128]{2,0,1:T(8,128)}), f32[8,128,128]{2,0,1:T(8,128)S(1)}, u32[]{:S(2)}, u32[]{:S(2)}) async-start(f32[8,128,128]{2,0,1:T(8,128)} %copy.167), calls=%async_computation.1 | async-start | bytes 1048576 | tf_op jit(solution)/shard_map/all_to_all | solution.py:142
  92.8 3.9 copy-start.9
  100.3 3.5 copy-start.4
  102.2 3.2 copy-start
  102.2 3.2 copy-start.2
  122.6 36.9 %all-to-all-start.2 = ((f32[8,128,128]{2,0,1:T(8,128)}), f32[8,128,128]{2,0,1:T(8,128)S(1)}, u32[]{:S(2)}, u32[]{:S(2)}) async-start(f32[8,128,128]{2,0,1:T(8,128)} %copy.189), calls=%async_computation.2 | async-start | bytes 1048576 | tf_op jit(solution)/shard_map/all_to_all | solution.py:123
  246.6 9.6 %copy-start.16 = (f32[8]{0:T(128)}, f32[8]{0:T(128)S(1)}, u32[]{:S(2)}) copy-start(f32[8]{0:T(128)S(1)} %div.44) | copy-start | bytes 100
  318.8 9.7 %copy-start.18 = (f32[8]{0:T(128)}, f32[8]{0:T(128)S(1)}, u32[]{:S(2)}) copy-start(f32[8]{0:T(128)S(1)} %psum.30) | copy-start | bytes 100
  318.8 14.8 %copy-start.15 = (pred[640]{0:T(1024)(128)(4,1)S(1)}, pred[640]{0:T(1024)(128)(4,1)}, u32[]{:S(2)}) copy-start(pred[640]{0:T(1024)(128)(4,1)} %copy-done.14) | copy-start | bytes 1924
  335.5 21.4 %all-to-all-start.3 = ((f32[8,128,128]{2,0,1:T(8,128)}), f32[8,128,128]{2,0,1:T(8,128)S(1)}, u32[]{:S(2)}, u32[]{:S(2)}) async-start(f32[8,128,128]{2,0,1:T(8,128)} %copy.197), calls=%async_computation.3 | async-start | bytes 1048576 | tf_op jit(solution)/shard_map/all_to_all | solution.py:142
  356.2 3.3 copy-start.7
  364.1 3.5 copy-start.5
  365.9 3.2 copy-start.1
  366.0 3.2 copy-start.3
  372.5 9.6 %copy-start.8 = (pred[125,64,2]{0,2,1:T(4,128)(4,1)S(1)}, pred[125,64,2]{0,2,1:T(4,128)(4,1)}, u32[]{:S(2)}) copy-start(pred[125,64,2]{0,2,1:T(4,128)(4,1)} %copy-done.6) | copy-start | bytes 48004
  385.4 36.9 %all-to-all-start.4 = ((f32[8,128,128]{2,0,1:T(8,128)}), f32[8,128,128]{2,0,1:T(8,128)S(1)}, u32[]{:S(2)}, u32[]{:S(2)}) async-start(f32[8,128,128]{2,0,1:T(8,128)} %copy.217), calls=%async_computation.4 | async-start | bytes 1048576 | tf_op jit(solution)/shard_map/all_to_all | solution.py:123
  434.9 74.4 %copy-start.19 = (f32[8]{0:T(128)S(1)}, f32[8]{0:T(128)}, u32[]{:S(2)}) copy-start(f32[8]{0:T(128)} %copy-done.18) | copy-start | bytes 100
  434.9 74.4 %copy-start.17 = (f32[8]{0:T(128)S(1)}, f32[8]{0:T(128)}, u32[]{:S(2)}) copy-start(f32[8]{0:T(128)} %copy-done.16) | copy-start | bytes 100
where the time goes:
time: 551 us; the launch traced here: 541 us
  blocking collectives  197 us (36%)
  matrix products  125 us (23%)
  other arithmetic  94.9 us (17%)
  local copies, waits for them, and re-layouts  76.8 us (14%)
  starting transfers between devices  46.2 us (8%)
    psum x2, blocking collectives, norm_sum(): return lax.psum(jnp.sum(residual * precond, axis=1), 'dom')  130 us
    psum x1, blocking collectives, on_device(): lax.psum(jnp.sum(direction * applied, axis=1), 'dom')  67.2 us
    dot_general x3, matrix products, scatter_own(): jnp.einsum('ngew,vnge->vgw', own_hot, values.reshape(rows, NPE, pair_coun...  53.3 us
    all_to_all x3, starting transfers between devices, return_sums(): lax.all_to_all(pending, 'dom', split_axis=1, concat_axis=1, tiled=True)  31 us
    dot_general x2, matrix products, on_device(): jnp.einsum('ngew,vgw->vnge', own_hot, direction.reshape(gather_rows, pair...  30.6 us
    scatter-add x2, other arithmetic, on_device(): owned_rows.at[:, send_flat]  24.1 us
    sub x1, other arithmetic, on_device(): residual = residual - step_size[:, None] * applied  20 us
    unnamed x50, local copies, waits for them, and re-layouts  19.2 us
  transfers between devices with their start and end apart: 5, of which 0 were waited for; matrix products, arithmetic and copies ran while one was open for 20% of the time, Pallas kernels for 0%

commit v1 on v0

v1 whole, which is shorter than its diff:
```python
import functools

import jax
import jax.numpy as jnp
import numpy as np
from jax import lax
from jax.experimental import pallas as pl
from jax.experimental.pallas import tpu as pltpu
from jax.sharding import PartitionSpec as P

MESH = pl.DeviceIdType.MESH
F32 = jnp.float32
BF16 = jnp.bfloat16
NV = 8
NPE = 125
LANES = 128
GROUP = 8
KEYS = 144
BLOCK = 16


def gll_matrix():
    points = np.array([-1.0, -np.sqrt(3.0 / 7.0), 0.0, np.sqrt(3.0 / 7.0), 1.0])
    weights = np.array(
        [
            1.0 / np.prod([points[column] - points[other] for other in range(5) if other != column])
            for column in range(5)
        ]
    )
    matrix = np.zeros((5, 5))
    for row_index in range(5):
        for column in range(5):
            if row_index != column:
                matrix[row_index, column] = (
                    weights[column] / weights[row_index] / (points[row_index] - points[column])
                )
        matrix[row_index, row_index] = -np.sum(matrix[row_index])
    return matrix


def split_numpy(matrix):
    single = matrix.astype(np.float32)
    high = single.astype(jnp.bfloat16)
    low = (single - high.astype(np.float32)).astype(jnp.bfloat16)
    return high, low


def operator_matrices():
    matrix = gll_matrix().astype(np.float32)
    eye = np.eye(5, dtype=np.float32)

    def along(small):
        full = np.zeros((3, LANES, LANES), np.float32)
        full[0, :NPE, :NPE] = np.kron(np.kron(small, eye), eye)
        full[1, :NPE, :NPE] = np.kron(np.kron(eye, small), eye)
        full[2, :NPE, :NPE] = np.kron(np.kron(eye, eye), small)
        return full

    grad = np.concatenate([full.T for full in along(matrix)], axis=1)
    first_high, first_low = split_numpy(grad)
    first = np.concatenate([first_high, first_low], axis=1)
    first = np.concatenate([first, first], axis=0)
    back = np.concatenate(list(along(matrix)), axis=0)
    second = np.concatenate(split_numpy(back), axis=1)
    second = np.concatenate([second, second], axis=0)
    square = np.concatenate(list(along(matrix * matrix)), axis=0)
    third = np.concatenate(split_numpy(square), axis=1)
    third = np.concatenate([third, third], axis=0)
    return first, second, third


def split(value):
    high = value.astype(BF16)
    return high, (value - high.astype(F32)).astype(BF16)


def parts(value):
    return jnp.concatenate(split(value), axis=1)


def matmul(left, right):
    return lax.dot_general(left, right, (((1,), (0,)), ((), ())), preferred_element_type=F32)


def matmul_nt(left, right):
    return lax.dot_general(left, right, (((1,), (1,)), ((), ())), preferred_element_type=F32)


def flipped(rank, bit):
    return rank + bit - 2 * bit * ((rank // bit) % 2)


def kernel(
    devices,
    density,
    peer_rank,
    right,
    stiffness,
    mass,
    region,
    nodes,
    send_nodes,
    first,
    second,
    third,
    solution_out,
    residual_out,
    stiff,
    mass_term,
    node_table,
    key_table,
    hot,
    diag_term,
    diagonal,
    z_own,
    w_own,
    q_own,
    p_own,
    lane_hot,
    lane_hot_t,
    values,
    ghost,
    compact,
    outgoing,
    incoming_0,
    incoming_1,
    incoming_2,
    incoming_3,
    incoming_4,
    ordered,
    send_sem,
    recv_sem,
    partial,
    near_in,
    far_in,
    near_send,
    near_recv,
    far_send,
    far_recv,
):
    me = lax.axis_index("dom")
    incoming = [incoming_0, incoming_1, incoming_2, incoming_3, incoming_4]
    elems = nodes.shape[1]
    pairs = elems // 2
    edge_pairs = pairs // 2
    peers = send_nodes.shape[1]
    live = peers * LANES
    run = live // edge_pairs
    bits = devices.bit_length() - 1
    candidates = [(me + 1) % devices, (me + devices - 1) % devices]
    candidates += [flipped(me, 2**k) for k in range(1, bits)]
    arrival = [1, 0] + list(range(2, len(candidates)))
    far_count = devices // GROUP
    near = [me - me % GROUP + (me + step) % GROUP for step in range(1, GROUP)]
    far = [(me + step * GROUP) % devices for step in range(1, far_count)]

    barrier = pltpu.get_barrier_semaphore()
    for other in candidates + near + far:
        pl.semaphore_signal(barrier, inc=1, device_id=(other,), device_id_type=MESH)

    stiff[...] = jnp.zeros_like(stiff)
    mass_term[...] = jnp.zeros_like(mass_term)
    node_table[...] = jnp.zeros_like(node_table)
    lane_row = lax.broadcasted_iota(jnp.int32, (1, LANES), 1)
    for half in range(elems // LANES):
        columns = slice(half * LANES, (half + 1) * LANES)
        for axis in range(3):
            stiff[columns, axis * LANES : axis * LANES + NPE] = stiffness[axis, :, columns].T
        tag = region[:, columns]
        weight = jnp.where(
            tag == 0, density[0], jnp.where(tag == 1, density[1], density[2])
        )
        mass_term[columns, :NPE] = (mass[:, columns] * weight).T
        node_table[columns, :NPE] = nodes[:, columns].T
    table = node_table[...]
    own_count = pairs * LANES
    pair_of = lax.broadcasted_iota(jnp.int32, table.shape, 0) // 2
    key = jnp.where(
        table < own_count, table & (LANES - 1), LANES + ((table - run * pair_of) & (LANES - 1))
    )
    key_table[...] = jnp.where(
        lax.broadcasted_iota(jnp.int32, table.shape, 1) < NPE, key, 255
    )
    sends = send_nodes[0]
    send_row = jnp.concatenate([sends[p : p + 1, :] for p in range(peers)], axis=1)
    send_lane = send_row & (LANES - 1)
    send_window = jnp.broadcast_to(send_row // LANES, (NV, live))
    picks = (
        lax.broadcasted_iota(jnp.int32, (LANES, live), 0) == send_lane
    ).astype(F32).astype(BF16)
    lane_hot[:LANES] = picks
    lane_hot[LANES:] = picks
    lane_hot_t[:, :live] = picks
    lane_hot_t[:, live:] = picks
    ghost[...] = jnp.zeros_like(ghost)

    diag_out = matmul(parts(stiff[...]), third[...])
    diag_term[...] = diag_out[:, :LANES] + diag_out[:, LANES:] + mass_term[...]

    def scatter_pair(pair, both):
        rows = jnp.concatenate([both, both - both.astype(BF16).astype(F32)], axis=0).astype(BF16)
        summed = matmul_nt(rows, hot[pair])
        return summed[:NV] + summed[NV:]

    def gather_ghosts():
        slots = [jnp.zeros((NV, LANES), F32) for _ in range(peers)]
        lane = lax.broadcasted_iota(jnp.int32, (NV, LANES), 1)
        for pair in range(edge_pairs):
            base = pair * run
            begin = base % LANES
            row = ghost[pair]
            if begin:
                row = pltpu.roll(row, begin, 1)
            here, last = base // LANES, (base + run - 1) // LANES
            if here == last:
                slots[here] = slots[here] + row
            else:
                slots[here] = slots[here] + jnp.where(lane >= begin, row, 0.0)
                slots[last] = slots[last] + jnp.where(lane < begin, row, 0.0)
        return slots

    def remote(phase, j):
        return pltpu.make_async_remote_copy(
            src_ref=outgoing.at[phase, j],
            dst_ref=incoming[phase].at[arrival[j]],
            send_sem=send_sem.at[phase, j],
            recv_sem=recv_sem.at[phase, arrival[j]],
            device_id=(candidates[j],),
            device_id_type=MESH,
        )

    def slot_of(j):
        slot = jnp.int32(0)
        for p in range(peers):
            slot = jnp.where(peer_rank[0, p] == candidates[j], p, slot)
        return slot

    def candidate_of(p):
        found = jnp.int32(0)
        for j in range(len(candidates)):
            found = jnp.where(peer_rank[0, p] == candidates[j], j, found)
        return found

    slots_of = [slot_of(j) for j in range(len(candidates))]
    candidates_of = [candidate_of(p) for p in range(peers)]

    def send(phase, slots):
        for p in range(peers):
            compact[phase, p] = slots[p]
        for j in range(len(candidates)):
            outgoing[phase, j] = compact[phase, slots_of[j]]
            remote(phase, j).start()

    def receive(phase):
        for j in range(len(candidates)):
            remote(phase, j).wait_recv()
        return [incoming[phase][candidates_of[p]] for p in range(peers)]

    def add_returned(own, received):
        value = jnp.concatenate(received, axis=1)

        def body(block, carry):
            rows = []
            for i in range(BLOCK):
                rows.append(jnp.where(send_window == block * BLOCK + i, value, 0.0))
            picked = parts(jnp.concatenate(rows, axis=0))
            at = pl.ds(pl.multiple_of(block * BLOCK * NV, BLOCK * NV), BLOCK * NV)
            own[at, :] = own[at, :] + matmul_nt(picked, lane_hot_t[...])
            return carry

        lax.fori_loop(0, pairs // BLOCK, body, 0)

    def pick_shared(own):
        def body(block, total):
            at = pl.ds(pl.multiple_of(block * BLOCK * NV, BLOCK * NV), BLOCK * NV)
            spread = matmul(parts(own[at, :]), lane_hot[...])
            for i in range(BLOCK):
                total = total + jnp.where(
                    send_window == block * BLOCK + i, spread[i * NV : (i + 1) * NV], 0.0
                )
            return total

        total = lax.fori_loop(0, pairs // BLOCK, body, jnp.zeros((NV, live), F32))
        return [total[:, p * LANES : (p + 1) * LANES] for p in range(peers)]

    def build_and_scatter(edge):
        def body(index, carry):
            pair = index if edge else index + edge_pairs
            count = KEYS if edge else LANES
            both = pl.ds(2 * pair, 1), pl.ds(2 * pair + 1, 1)
            keys = jnp.concatenate([key_table[both[0], :], key_table[both[1], :]], axis=1)
            rows = lax.broadcasted_iota(jnp.int32, (count, 2 * LANES), 0)
            hot[pair, :count] = (rows == keys).astype(F32).astype(BF16)
            term = jnp.concatenate([diag_term[both[0], :], diag_term[both[1], :]], axis=1)
            summed = scatter_pair(pair, jnp.broadcast_to(term, (NV, 2 * LANES)))
            at = pl.ds(pl.multiple_of(pair * NV, NV), NV)
            diagonal[at, :] = summed[:, :LANES]
            if edge:
                ghost[pair, :, : KEYS - LANES] = summed[:, LANES:]
            return carry

        lax.fori_loop(0, edge_pairs, body, 0, unroll=4)

    def apply_blocks(source, target, edge, total):
        def body(index, total):
            block = index if edge else index + edge_pairs // BLOCK
            for i in range(BLOCK):
                pair = block * BLOCK + i
                own = source[pl.ds(pl.multiple_of(pair * NV, NV), NV), :]
                if edge:
                    base = pair * run
                    lane = lax.broadcasted_iota(jnp.int32, (NV, LANES), 1)
                    begin = base % LANES
                    received = jnp.where(
                        lane >= begin, ordered[base // LANES], ordered[(base + run - 1) // LANES]
                    )
                for side in range(2):
                    node = jnp.broadcast_to(node_table[pl.ds(2 * pair + side, 1), :], (NV, LANES))
                    lanes = node & (LANES - 1)
                    picked = jnp.take_along_axis(own, lanes, axis=1, mode="promise_in_bounds")
                    if edge:
                        remote_value = jnp.take_along_axis(
                            received, lanes, axis=1, mode="promise_in_bounds"
                        )
                        picked = jnp.where(node < own_count, picked, remote_value)
                    values[(2 * i + side) * NV : (2 * i + side + 1) * NV, :] = picked
            value = values[...]
            grad = matmul(parts(value), first[...])
            flux = grad[:, : 3 * LANES] + grad[:, 3 * LANES :]
            scaled = []
            masses = []
            for i in range(2 * BLOCK):
                at = pl.ds(block * 2 * BLOCK + i, 1)
                scaled.append(flux[i * NV : (i + 1) * NV] * stiff[at, :])
                masses.append(jnp.broadcast_to(mass_term[at, :], (NV, LANES)))
            back = matmul(parts(jnp.concatenate(scaled, axis=0)), second[...])
            result = back[:, :LANES] + back[:, LANES:] + jnp.concatenate(masses, axis=0) * value
            product = value * result
            for i in range(2 * BLOCK):
                total = total + product[i * NV : (i + 1) * NV]
            for i in range(BLOCK):
                pair = block * BLOCK + i
                low = 2 * i * NV
                both = jnp.concatenate(
                    [result[low : low + NV], result[low + NV : low + 2 * NV]], axis=1
                )
                rows = jnp.concatenate(
                    [both, both - both.astype(BF16).astype(F32)], axis=0
                ).astype(BF16)
                count = KEYS if edge else LANES
                summed = matmul_nt(rows, hot[pair, :count])
                summed = summed[:NV] + summed[NV:]
                target[pl.ds(pl.multiple_of(pair * NV, NV), NV), :] = summed[:, :LANES]
                if edge:
                    ghost[pair, :, : KEYS - LANES] = summed[:, LANES:]
            return total

        return lax.fori_loop(0, edge_pairs // BLOCK, body, total)

    def over_pairs(step, total):
        def body(pair, total):
            return step(pair, pl.ds(pl.multiple_of(pair * NV, NV), NV), total)

        return lax.fori_loop(0, pairs, body, total, unroll=8)

    zero = jnp.zeros((NV, LANES), F32)
    build_and_scatter(True)
    pl.semaphore_wait(barrier, len(candidates) + len(near) + len(far))
    send(0, gather_ghosts())
    build_and_scatter(False)
    add_returned(diagonal, receive(0))

    def begin(pair, at, total):
        value = right[:, pl.ds(pl.multiple_of(pair * LANES, LANES), LANES)]
        scaled = value / diagonal[at, :]
        z_own[at, :] = scaled
        return total + value * scaled

    sum_rz = over_pairs(begin, zero)

    def apply(source, target, phase):
        send(phase, pick_shared(source))
        total = apply_blocks(source, target, False, zero)
        for p, value in enumerate(receive(phase)):
            ordered[p] = value
        total = apply_blocks(source, target, True, total)
        send(phase + 1, gather_ghosts())
        return total

    sum_zw = apply(z_own, w_own, 1)
    add_returned(w_own, receive(2))

    def middle(pair, at, total):
        value = w_own[at, :]
        scaled = value / diagonal[at, :]
        q_own[at, :] = scaled
        return total + value * scaled

    sum_wq = over_pairs(middle, zero)
    sum_qp = apply(q_own, p_own, 3)

    lane = lax.broadcasted_iota(jnp.int32, (NV, LANES), 1)
    quarter = LANES // 4
    packed = zero
    for place, total in enumerate((sum_rz, sum_zw, sum_wq, sum_qp)):
        total = total + pltpu.roll(total, LANES // 2, 1)
        total = total + pltpu.roll(total, quarter, 1)
        packed = jnp.where(lane // quarter == place, total, packed)

    def near_copy(step):
        return pltpu.make_async_remote_copy(
            src_ref=partial.at[0],
            dst_ref=near_in.at[step],
            send_sem=near_send.at[step],
            recv_sem=near_recv.at[step],
            device_id=(near[step],),
            device_id_type=MESH,
        )

    def far_copy(step):
        return pltpu.make_async_remote_copy(
            src_ref=partial.at[1],
            dst_ref=far_in.at[step],
            send_sem=far_send.at[step],
            recv_sem=far_recv.at[step],
            device_id=(far[step],),
            device_id_type=MESH,
        )

    partial[0] = packed
    for step in range(len(near)):
        near_copy(step).start()
    for step in range(len(near)):
        near_copy(step).wait_recv()
        packed = packed + near_in[step]
    partial[1] = packed
    for step in range(len(far)):
        far_copy(step).start()
    add_returned(p_own, receive(4))
    for step in range(len(far)):
        far_copy(step).wait_recv()
        packed = packed + far_in[step]
    rz, zw, wq, qp = [
        jnp.sum(jnp.where(lane // quarter == place, packed, 0.0), axis=1, keepdims=True)
        for place in range(4)
    ]
    alpha = rz / zw
    new = rz - 2.0 * alpha * zw + alpha * alpha * wq
    ratio = 1.0 + new / rz
    second_alpha = new / (
        ratio * ratio * zw - 2.0 * alpha * ratio * wq + alpha * alpha * qp
    )
    outer = jnp.broadcast_to(alpha + second_alpha * ratio, (NV, LANES))
    inner = jnp.broadcast_to(alpha * second_alpha, (NV, LANES))

    def finish(pair, at, total):
        out = pl.ds(pl.multiple_of(pair * LANES, LANES), LANES)
        solution_out[:, out] = outer * z_own[at, :] - inner * q_own[at, :]
        residual_out[:, out] = right[:, out] - outer * w_own[at, :] + inner * p_own[at, :]
        return total

    over_pairs(finish, zero)
    for phase in range(5):
        for j in range(len(candidates)):
            remote(phase, j).wait_send()
    for step in range(len(near)):
        near_copy(step).wait_send()
    for step in range(len(far)):
        far_copy(step).wait_send()


def on_device(devices, right, stiffness, mass, region, density, elem_nodes, peer_rank, send_nodes):
    first, second, third = (jnp.asarray(matrix) for matrix in operator_matrices())
    own_count = right.shape[1]
    elems = elem_nodes.shape[1]
    pairs = elems // 2
    peers = send_nodes.shape[1]
    live = peers * LANES
    bits = devices.bit_length() - 1
    ways = bits + 1
    near_count, far_count = GROUP - 1, devices // GROUP - 1
    vmem = pl.BlockSpec(memory_space=pltpu.VMEM)
    smem = pl.BlockSpec(memory_space=pltpu.SMEM)
    owned = pltpu.VMEM((pairs * NV, LANES), F32)
    dma = pltpu.SemaphoreType.DMA
    return pl.pallas_call(
        functools.partial(kernel, devices),
        out_shape=(
            jax.ShapeDtypeStruct((NV, own_count), F32),
            jax.ShapeDtypeStruct((NV, own_count), F32),
        ),
        in_specs=[smem, smem] + [vmem] * 9,
        out_specs=(vmem, vmem),
        scratch_shapes=[
            pltpu.VMEM((elems, 3 * LANES), F32),
            pltpu.VMEM((elems, LANES), F32),
            pltpu.VMEM((elems, LANES), jnp.int32),
            pltpu.VMEM((elems, LANES), jnp.int32),
            pltpu.VMEM((pairs, KEYS, 2 * LANES), BF16),
            pltpu.VMEM((elems, LANES), F32),
            owned,
            owned,
            owned,
            owned,
            owned,
            pltpu.VMEM((2 * LANES, live), BF16),
            pltpu.VMEM((LANES, 2 * live), BF16),
            pltpu.VMEM((2 * BLOCK * NV, LANES), F32),
            pltpu.VMEM((pairs // 2, NV, LANES), F32),
            pltpu.VMEM((5, peers, NV, LANES), F32),
            pltpu.VMEM((5, ways, NV, LANES), F32),
            pltpu.VMEM((ways, NV, LANES), F32),
            pltpu.VMEM((ways, NV, LANES), F32),
            pltpu.VMEM((ways, NV, LANES), F32),
            pltpu.VMEM((ways, NV, LANES), F32),
            pltpu.VMEM((ways, NV, LANES), F32),
            pltpu.VMEM((peers, NV, LANES), F32),
            dma((5, ways)),
            dma((5, ways)),
            pltpu.VMEM((2, NV, LANES), F32),
            pltpu.VMEM((near_count, NV, LANES), F32),
            pltpu.VMEM((far_count, NV, LANES), F32),
            dma((near_count,)),
            dma((near_count,)),
            dma((far_count,)),
            dma((far_count,)),
        ],
        compiler_params=pltpu.CompilerParams(
            collective_id=0, has_side_effects=True, vmem_limit_bytes=48 * 1024 * 1024
        ),
    )(
        density,
        peer_rank,
        right,
        stiffness,
        mass,
        region.reshape(1, elems),
        elem_nodes,
        send_nodes,
        first,
        second,
        third,
    )


def solution(mesh):
    devices = mesh.shape["dom"]
    placed = (
        P(None, "dom"),
        P(None, None, "dom"),
        P(None, "dom"),
        P("dom"),
        P(),
        P(None, "dom"),
        P("dom", None),
        P("dom", None, None),
    )
    return jax.shard_map(
        functools.partial(on_device, devices),
        mesh=mesh,
        in_specs=placed,
        out_specs=(P(None, "dom"), P(None, "dom")),
        check_vma=False,
    )
```

time: 551 us -> 66 us (0.12); the launches traced: 541 us -> 65.7 us
  blocking collectives: 197 us -> 0 us
  matrix products: 125 us -> 0 us
  other arithmetic: 94.9 us -> 0 us
  local copies, waits for them, and re-layouts: 76.8 us -> 9.13 us
  Pallas kernels: 0 us -> 55.8 us
  starting transfers between devices: 46.2 us -> 0 us
    psum x3 -> x0, blocking collectives: 197 us -> none  [the longest x2 130 us: norm_sum(): return lax.psum(jnp.sum(residual * precond, axis=1), 'dom')]
    dot_general x40 -> x0, matrix products: 125 us -> none  [the longest x3 53.3 us: scatter_own(): jnp.einsum('ngew,vnge->vgw', own_hot, values.reshape(rows, NPE, pair_coun...]
    pallas_call x0 -> x1, Pallas kernels: none -> 55.8 us  [on_device(): pl.pallas_call(functools.partial(kernel, devices), out_shape=(jax.ShapeDt...]
    all_to_all x5 -> x0, starting transfers between devices: 46.2 us -> none  [the longest x3 31 us: return_sums(): lax.all_to_all(pending, 'dom', split_axis=1, concat_axis=1, tiled=True)]
    scatter-add x3 -> x0, other arithmetic: 28.8 us -> none  [the longest x2 24.1 us: on_device(): owned_rows.at[:, send_flat]]
    reduce_sum x5 -> x0, other arithmetic: 25.7 us -> none  [the longest x2 14.5 us: on_device(): jnp.sum(direction * applied, axis=1)]
    add x6 -> x0, local copies, waits for them, and re-layouts: 22.3 us -> none  [the longest x4 19.1 us: element_apply(): return result + mass_grid * gathered]
    sub x2 -> x0, other arithmetic: 20.2 us -> none  [the longest x1 20 us: on_device(): residual = residual - step_size[:, None] * applied]
  transfers between devices with their start and end apart: 5 -> 0, of which waited for: 0 -> 0; matrix products, arithmetic and copies ran while one was open for 20% -> 0% of each run, Pallas kernels for 0% -> 0%
where the time goes in v1:
time: 66 us; the launch traced here: 65.7 us
  Pallas kernels  55.8 us (85%)
  local copies, waits for them, and re-layouts  9.13 us (14%)
  between operations  0.68 us (1%)
    pallas_call x1, Pallas kernels, on_device(): pl.pallas_call(functools.partial(kernel, devices), out_shape=(jax.ShapeDt...  55.8 us
    unnamed x23, local copies, waits for them, and re-layouts  9.13 us

profile of v1, /device:TPU:1, one launch (start us, length us, event | category | flops | bytes accessed | tf_op | source)
XLA Modules:
  0.0 65.7 jit_solution(6715410775920165772)
XLA Ops:
  0.6 0.0 copy-start.7
  0.6 0.0 copy-start.8
  0.7 0.0 copy-start.9
  0.7 0.7 %copy.13.send_nodes = s32[1,5,128]{2,1,0:T(8,128)S(1)} copy(s32[1,5,128]{2,0,1:T(1,128)} %param.18) | data formatting | bytes 5120 | tf_op args[7]
  1.4 0.0 copy-done.7
  1.4 0.0 copy-done.8
  1.4 0.0 copy-done.9
  1.4 0.0 copy-start
  1.4 1.0 %copy-done = f32[8,16384]{1,0:T(8,128)S(1)} copy-done((f32[8,16384]{1,0:T(8,128)S(1)}, f32[8,16384]{1,0:T(8,128)}, u32[]{:S(2)}) %copy-start) | copy-done | bytes 524312
  2.4 0.0 copy-start.1
  2.4 1.0 %copy-done.1 = f32[3,125,256]{2,1,0:T(8,128)S(1)} copy-done((f32[3,125,256]{2,1,0:T(8,128)S(1)}, f32[3,125,256]{2,1,0:T(8,128)}, u32[]{:S(2)}) %copy-start.1) | copy-done | bytes 384024
  3.4 0.0 copy-start.2
  3.4 1.0 %copy-done.2 = bf16[768,256]{1,0:T(8,128)(2,1)S(1)} copy-done((bf16[768,256]{1,0:T(8,128)(2,1)S(1)}, bf16[768,256]{1,0:T(8,128)(2,1)}, u32[]{:S(2)}) %copy-start.2) | copy-done | bytes 393240
  4.4 0.0 copy-start.3
  4.4 1.0 %copy-done.3 = bf16[768,256]{1,0:T(8,128)(2,1)S(1)} copy-done((bf16[768,256]{1,0:T(8,128)(2,1)S(1)}, bf16[768,256]{1,0:T(8,128)(2,1)}, u32[]{:S(2)}) %copy-start.3) | copy-done | bytes 393240
  5.4 0.0 copy-start.4
  5.4 1.0 %copy-done.4 = bf16[256,768]{1,0:T(8,128)(2,1)S(1)} copy-done((bf16[256,768]{1,0:T(8,128)(2,1)S(1)}, bf16[256,768]{1,0:T(8,128)(2,1)}, u32[]{:S(2)}) %copy-start.4) | copy-done | bytes 393240
  6.4 0.0 copy-start.5
  6.4 0.9 %copy-done.5 = f32[125,256]{1,0:T(8,128)S(1)} copy-done((f32[125,256]{1,0:T(8,128)S(1)}, f32[125,256]{1,0:T(8,128)}, u32[]{:S(2)}) %copy-start.5) | copy-done | bytes 128024
  7.3 0.0 copy-start.6
  7.3 0.9 %copy-done.6 = s32[125,256]{1,0:T(8,128)S(1)} copy-done((s32[125,256]{1,0:T(8,128)S(1)}, s32[125,256]{1,0:T(8,128)}, u32[]{:S(2)}) %copy-start.6) | copy-done | bytes 128024
  8.2 55.8 %shard_map.122 = (f32[8,16384]{1,0:T(8,128)S(1)}, f32[8,16384]{1,0:T(8,128)S(1)}) custom-call(f32[3]{0:T(128)S(1)} %copy-done.8, s32[1,5]{1,0:T(1,128)S(1)} %copy-done.9, f32[8,16384]{1,0:T(8,128)S(1)} %copy-done, f32[3,125,256]{2,1,0:T(8,128)S(1)} %copy-done.1, f32[125,256]{1,0:T(8,128)S(1)} %copy-done.5, s32[1,256]{1,0:T(1,128)S(1)} %bitcast.1, ...), custom_call_target="tpu_custom_call" | custom-call | tf_op jit(solution)/shard_map/pallas_call | solution.py:486
  64.1 0.8 %copy.16 = f32[8,16384]{1,0:T(8,128)} copy(f32[8,16384]{1,0:T(8,128)S(1)} %get-tuple-element.4) | data formatting | bytes 1048576
  64.9 0.8 %copy.17 = f32[8,16384]{1,0:T(8,128)} copy(f32[8,16384]{1,0:T(8,128)S(1)} %get-tuple-element.5) | data formatting | bytes 1048576
Async XLA Ops:
  0.6 0.7 %copy-start.7 = (s32[256]{0:T(256)S(1)}, s32[256]{0:T(256)}, u32[]{:S(2)}) copy-start(s32[256]{0:T(256)} %param.14) | copy-start | bytes 3076
  0.6 0.7 %copy-start.8 = (f32[3]{0:T(128)S(1)}, f32[3]{0:T(128)}, u32[]{:S(2)}) copy-start(f32[3]{0:T(128)} %density.1) | copy-start | bytes 40
  0.7 0.7 %copy-start.9 = (s32[1,5]{1,0:T(1,128)S(1)}, s32[1,5]{1,0:T(1,128)}, u32[]{:S(2)}) copy-start(s32[1,5]{1,0:T(1,128)} %peer_rank.1) | copy-start | bytes 64
  1.4 1.0 %copy-start = (f32[8,16384]{1,0:T(8,128)S(1)}, f32[8,16384]{1,0:T(8,128)}, u32[]{:S(2)}) copy-start(f32[8,16384]{1,0:T(8,128)} %right.1) | copy-start | bytes 1572868
  2.4 1.0 %copy-start.1 = (f32[3,125,256]{2,1,0:T(8,128)S(1)}, f32[3,125,256]{2,1,0:T(8,128)}, u32[]{:S(2)}) copy-start(f32[3,125,256]{2,1,0:T(8,128)} %stiffness.1) | copy-start | bytes 1152004
  3.4 1.0 %copy-start.2 = (bf16[768,256]{1,0:T(8,128)(2,1)S(1)}, bf16[768,256]{1,0:T(8,128)(2,1)}, u32[]{:S(2)}) copy-start(bf16[768,256]{1,0:T(8,128)(2,1)} %constant.8.clone.third) | copy-start | bytes 1179652
  4.4 1.0 %copy-start.3 = (bf16[768,256]{1,0:T(8,128)(2,1)S(1)}, bf16[768,256]{1,0:T(8,128)(2,1)}, u32[]{:S(2)}) copy-start(bf16[768,256]{1,0:T(8,128)(2,1)} %constant.7.clone.second) | copy-start | bytes 1179652
  5.4 1.0 %copy-start.4 = (bf16[256,768]{1,0:T(8,128)(2,1)S(1)}, bf16[256,768]{1,0:T(8,128)(2,1)}, u32[]{:S(2)}) copy-start(bf16[256,768]{1,0:T(8,128)(2,1)} %constant.6.clone.first) | copy-start | bytes 1179652
  6.4 0.9 %copy-start.5 = (f32[125,256]{1,0:T(8,128)S(1)}, f32[125,256]{1,0:T(8,128)}, u32[]{:S(2)}) copy-start(f32[125,256]{1,0:T(8,128)} %mass.1) | copy-start | bytes 384004
  7.3 0.9 %copy-start.6 = (s32[125,256]{1,0:T(8,128)S(1)}, s32[125,256]{1,0:T(8,128)}, u32[]{:S(2)}) copy-start(s32[125,256]{1,0:T(8,128)} %nodes.1) | copy-start | bytes 384004

commit v2 on v1

--- a/solution.py
+++ b/solution.py
@@ -17,6 +17,7 @@
 GROUP = 8
 KEYS = 144
 BLOCK = 16
+WIDE = 32
 
 
 def gll_matrix():
@@ -94,6 +95,17 @@
     devices,
     density,
     peer_rank,
+    right_in,
+    stiffness_in,
+    mass_in,
+    region_in,
+    nodes_in,
+    send_in,
+    first_in,
+    second_in,
+    third_in,
+    solution_out,
+    residual_out,
     right,
     stiffness,
     mass,
@@ -103,8 +115,7 @@
     first,
     second,
     third,
-    solution_out,
-    residual_out,
+    in_sem,
     stiff,
     mass_term,
     node_table,
@@ -117,8 +128,9 @@
     q_own,
     p_own,
     lane_hot,
-    lane_hot_t,
-    values,
+    back_hot,
+    same_hot,
+    diag_rows,
     ghost,
     compact,
     outgoing,
@@ -143,7 +155,7 @@
     elems = nodes.shape[1]
     pairs = elems // 2
     edge_pairs = pairs // 2
-    peers = send_nodes.shape[1]
+    peers = send_nodes.shape[0]
     live = peers * LANES
     run = live // edge_pairs
     bits = devices.bit_length() - 1
@@ -154,23 +166,23 @@
     near = [me - me % GROUP + (me + step) % GROUP for step in range(1, GROUP)]
     far = [(me + step * GROUP) % devices for step in range(1, far_count)]
 
+    sources = [nodes_in, send_in, stiffness_in, region_in, mass_in, third_in, right_in, first_in, second_in]
+    places = [nodes, send_nodes, stiffness, region, mass, third, right, first, second]
+    loads = [
+        pltpu.make_async_copy(source, place, in_sem.at[index])
+        for index, (source, place) in enumerate(zip(sources, places))
+    ]
+    for load in loads:
+        load.start()
+
     barrier = pltpu.get_barrier_semaphore()
     for other in candidates + near + far:
         pl.semaphore_signal(barrier, inc=1, device_id=(other,), device_id_type=MESH)
 
-    stiff[...] = jnp.zeros_like(stiff)
-    mass_term[...] = jnp.zeros_like(mass_term)
     node_table[...] = jnp.zeros_like(node_table)
-    lane_row = lax.broadcasted_iota(jnp.int32, (1, LANES), 1)
-    for half in range(elems // LANES):
-        columns = slice(half * LANES, (half + 1) * LANES)
-        for axis in range(3):
-            stiff[columns, axis * LANES : axis * LANES + NPE] = stiffness[axis, :, columns].T
-        tag = region[:, columns]
-        weight = jnp.where(
-            tag == 0, density[0], jnp.where(tag == 1, density[1], density[2])
-        )
-        mass_term[columns, :NPE] = (mass[:, columns] * weight).T
+    loads[0].wait()
+    halves = [slice(half * LANES, (half + 1) * LANES) for half in range(elems // LANES)]
+    for columns in halves:
         node_table[columns, :NPE] = nodes[:, columns].T
     table = node_table[...]
     own_count = pairs * LANES
@@ -180,30 +192,29 @@
     )
     key_table[...] = jnp.where(
         lax.broadcasted_iota(jnp.int32, table.shape, 1) < NPE, key, 255
-    )
-    sends = send_nodes[0]
-    send_row = jnp.concatenate([sends[p : p + 1, :] for p in range(peers)], axis=1)
-    send_lane = send_row & (LANES - 1)
-    send_window = jnp.broadcast_to(send_row // LANES, (NV, live))
-    picks = (
-        lax.broadcasted_iota(jnp.int32, (LANES, live), 0) == send_lane
-    ).astype(F32).astype(BF16)
-    lane_hot[:LANES] = picks
-    lane_hot[LANES:] = picks
-    lane_hot_t[:, :live] = picks
-    lane_hot_t[:, live:] = picks
+    ).astype(F32)
+    stiff[...] = jnp.zeros_like(stiff)
+    mass_term[...] = jnp.zeros_like(mass_term)
+    for load in loads[1:6]:
+        load.wait()
+    for columns in halves:
+        for axis in range(3):
+            stiff[columns, axis * LANES : axis * LANES + NPE] = stiffness[axis, :, columns].T
+        tag = region[:, columns]
+        weight = jnp.where(tag == 0, density[0], jnp.where(tag == 1, density[1], density[2]))
+        mass_term[columns, :NPE] = (mass[:, columns] * weight).T
     ghost[...] = jnp.zeros_like(ghost)
 
     diag_out = matmul(parts(stiff[...]), third[...])
     diag_term[...] = diag_out[:, :LANES] + diag_out[:, LANES:] + mass_term[...]
 
-    def scatter_pair(pair, both):
+    def scatter_pair(pair, both, count):
         rows = jnp.concatenate([both, both - both.astype(BF16).astype(F32)], axis=0).astype(BF16)
-        summed = matmul_nt(rows, hot[pair])
+        summed = matmul_nt(rows, hot[pair, :count])
         return summed[:NV] + summed[NV:]
 
     def gather_ghosts():
-        slots = [jnp.zeros((NV, LANES), F32) for _ in range(peers)]
+        sums = [jnp.zeros((NV, LANES), F32) for _ in range(peers)]
         lane = lax.broadcasted_iota(jnp.int32, (NV, LANES), 1)
         for pair in range(edge_pairs):
             base = pair * run
@@ -213,11 +224,11 @@
                 row = pltpu.roll(row, begin, 1)
             here, last = base // LANES, (base + run - 1) // LANES
             if here == last:
-                slots[here] = slots[here] + row
+                sums[here] = sums[here] + row
             else:
-                slots[here] = slots[here] + jnp.where(lane >= begin, row, 0.0)
-                slots[last] = slots[last] + jnp.where(lane < begin, row, 0.0)
-        return slots
+                sums[here] = sums[here] + jnp.where(lane >= begin, row, 0.0)
+                sums[last] = sums[last] + jnp.where(lane < begin, row, 0.0)
+        return sums
 
     def remote(phase, j):
         return pltpu.make_async_remote_copy(
@@ -244,9 +255,9 @@
     slots_of = [slot_of(j) for j in range(len(candidates))]
     candidates_of = [candidate_of(p) for p in range(peers)]
 
-    def send(phase, slots):
+    def send(phase, slot_values):
         for p in range(peers):
-            compact[phase, p] = slots[p]
+            compact[phase, p] = slot_values[p]
         for j in range(len(candidates)):
             outgoing[phase, j] = compact[phase, slots_of[j]]
             remote(phase, j).start()
@@ -258,52 +269,98 @@
 
     def add_returned(own, received):
         value = jnp.concatenate(received, axis=1)
+        high = value.astype(BF16).astype(F32)
+        low = jnp.concatenate([value - high] * 2, axis=0).astype(BF16)
+        high = jnp.concatenate([high] * 2, axis=0).astype(BF16)
+        window = jnp.broadcast_to((send_row // LANES).astype(F32), (2 * NV, live)).astype(BF16)
+        second_row = lax.broadcasted_iota(jnp.int32, (2 * NV, live), 0) // NV
+        none = jnp.zeros((2 * NV, live), BF16)
 
         def body(block, carry):
-            rows = []
-            for i in range(BLOCK):
-                rows.append(jnp.where(send_window == block * BLOCK + i, value, 0.0))
-            picked = parts(jnp.concatenate(rows, axis=0))
-            at = pl.ds(pl.multiple_of(block * BLOCK * NV, BLOCK * NV), BLOCK * NV)
-            own[at, :] = own[at, :] + matmul_nt(picked, lane_hot_t[...])
+            high_rows, low_rows = [], []
+            for i in range(WIDE // 2):
+                number = (second_row + (block * WIDE + 2 * i)).astype(F32).astype(BF16)
+                found = window == number
+                high_rows.append(jnp.where(found, high, none))
+                low_rows.append(jnp.where(found, low, none))
+            at = pl.ds(pl.multiple_of(block * WIDE * NV, WIDE * NV), WIDE * NV)
+            summed = matmul(jnp.concatenate(high_rows + low_rows, axis=0), back_hot[...])
+            own[at, :] = own[at, :] + (summed[: WIDE * NV] + summed[WIDE * NV :])
             return carry
 
-        lax.fori_loop(0, pairs // BLOCK, body, 0)
-
-    def pick_shared(own):
+        lax.fori_loop(0, pairs // WIDE, body, 0)
+
+    def pick_shared(load):
         def body(block, total):
-            at = pl.ds(pl.multiple_of(block * BLOCK * NV, BLOCK * NV), BLOCK * NV)
-            spread = matmul(parts(own[at, :]), lane_hot[...])
-            for i in range(BLOCK):
+            spread = matmul(parts(load(block)), lane_hot[...])
+            for i in range(WIDE):
                 total = total + jnp.where(
-                    send_window == block * BLOCK + i, spread[i * NV : (i + 1) * NV], 0.0
+                    send_window == block * WIDE + i, spread[i * NV : (i + 1) * NV], 0.0
                 )
             return total
 
-        total = lax.fori_loop(0, pairs // BLOCK, body, jnp.zeros((NV, live), F32))
-        return [total[:, p * LANES : (p + 1) * LANES] for p in range(peers)]
+        return lax.fori_loop(0, pairs // WIDE, body, jnp.zeros((NV, live), F32))
+
+    def owned_rows(own):
+        def load(block):
+            return own[pl.ds(pl.multiple_of(block * WIDE * NV, WIDE * NV), WIDE * NV), :]
+
+        return load
+
+    def right_rows(block):
+        base = block * WIDE * LANES
+        return jnp.concatenate(
+            [
+                right[:, pl.ds(pl.multiple_of(base + i * LANES, LANES), LANES)]
+                for i in range(WIDE)
+            ],
+            axis=0,
+        )
+
+    def pick_diagonal():
+        spread = matmul(parts(diag_rows[...]), lane_hot[...])
+        number = lax.broadcasted_iota(jnp.int32, (pairs, live), 0)
+        found = jnp.where(number == send_row // LANES, spread, 0.0)
+        return jnp.broadcast_to(jnp.sum(found, axis=0, keepdims=True), (NV, live))
+
+    def add_shared(shared, received):
+        value = jnp.concatenate(received, axis=1)
+        rows = jnp.concatenate([value, value - value.astype(BF16).astype(F32)], axis=0).astype(BF16)
+        summed = matmul(rows, same_hot[...])
+        return shared + (summed[:NV] + summed[NV:])
+
+    def slots(value):
+        return [value[:, p * LANES : (p + 1) * LANES] for p in range(peers)]
 
     def build_and_scatter(edge):
+        count = KEYS if edge else LANES
+        row_of = lax.broadcasted_iota(jnp.int32, (16, 2 * LANES), 0)
+        one, none = jnp.ones((16, 2 * LANES), BF16), jnp.zeros((16, 2 * LANES), BF16)
+
         def body(index, carry):
             pair = index if edge else index + edge_pairs
-            count = KEYS if edge else LANES
             both = pl.ds(2 * pair, 1), pl.ds(2 * pair + 1, 1)
             keys = jnp.concatenate([key_table[both[0], :], key_table[both[1], :]], axis=1)
-            rows = lax.broadcasted_iota(jnp.int32, (count, 2 * LANES), 0)
-            hot[pair, :count] = (rows == keys).astype(F32).astype(BF16)
+            keys = jnp.broadcast_to(keys, (16, 2 * LANES)).astype(BF16)
+            for tile in range(count // 16):
+                number = (row_of + 16 * tile).astype(F32).astype(BF16)
+                hot[pair, 16 * tile : 16 * tile + 16] = jnp.where(keys == number, one, none)
             term = jnp.concatenate([diag_term[both[0], :], diag_term[both[1], :]], axis=1)
-            summed = scatter_pair(pair, jnp.broadcast_to(term, (NV, 2 * LANES)))
+            summed = scatter_pair(pair, jnp.broadcast_to(term, (NV, 2 * LANES)), count)
             at = pl.ds(pl.multiple_of(pair * NV, NV), NV)
             diagonal[at, :] = summed[:, :LANES]
+            diag_rows[pl.ds(pair, 1), :] = summed[:1, :LANES]
             if edge:
                 ghost[pair, :, : KEYS - LANES] = summed[:, LANES:]
             return carry
 
         lax.fori_loop(0, edge_pairs, body, 0, unroll=4)
 
-    def apply_blocks(source, target, edge, total):
-        def body(index, total):
-            block = index if edge else index + edge_pairs // BLOCK
+    def apply_blocks(source, target, begin_block, end_block, total):
+        edge = begin_block < edge_pairs // BLOCK
+
+        def body(block, total):
+            gathered = []
             for i in range(BLOCK):
                 pair = block * BLOCK + i
                 own = source[pl.ds(pl.multiple_of(pair * NV, NV), NV), :]
@@ -323,8 +380,8 @@
                             received, lanes, axis=1, mode="promise_in_bounds"
                         )
                         picked = jnp.where(node < own_count, picked, remote_value)
-                    values[(2 * i + side) * NV : (2 * i + side + 1) * NV, :] = picked
-            value = values[...]
+                    gathered.append(picked)
+            value = jnp.concatenate(gathered, axis=0)
             grad = matmul(parts(value), first[...])
             flux = grad[:, : 3 * LANES] + grad[:, 3 * LANES :]
             scaled = []
@@ -344,18 +401,13 @@
                 both = jnp.concatenate(
                     [result[low : low + NV], result[low + NV : low + 2 * NV]], axis=1
                 )
-                rows = jnp.concatenate(
-                    [both, both - both.astype(BF16).astype(F32)], axis=0
-                ).astype(BF16)
-                count = KEYS if edge else LANES
-                summed = matmul_nt(rows, hot[pair, :count])
-                summed = summed[:NV] + summed[NV:]
+                summed = scatter_pair(pair, both, KEYS if edge else LANES)
                 target[pl.ds(pl.multiple_of(pair * NV, NV), NV), :] = summed[:, :LANES]
                 if edge:
                     ghost[pair, :, : KEYS - LANES] = summed[:, LANES:]
             return total
 
-        return lax.fori_loop(0, edge_pairs // BLOCK, body, total)
+        return lax.fori_loop(begin_block, end_block, body, total)
 
     def over_pairs(step, total):
         def body(pair, total):
@@ -367,8 +419,31 @@
     build_and_scatter(True)
     pl.semaphore_wait(barrier, len(candidates) + len(near) + len(far))
     send(0, gather_ghosts())
+
+    send_row = jnp.concatenate([send_nodes[p] for p in range(peers)], axis=1)
+    send_window = jnp.broadcast_to(send_row // LANES, (NV, live))
+    lane_number = lax.broadcasted_iota(jnp.int32, (LANES, live), 0)
+    picks = (lane_number == (send_row & (LANES - 1))).astype(F32).astype(BF16)
+    lane_hot[:LANES] = picks
+    lane_hot[LANES:] = picks
+    lane_number = lax.broadcasted_iota(jnp.int32, (LANES, LANES), 1)
+    for p in range(peers):
+        column = jnp.broadcast_to(send_nodes[p], (LANES, LANES)).T
+        rows = slice(p * LANES, (p + 1) * LANES)
+        back_hot[rows] = (lane_number == (column & (LANES - 1))).astype(F32).astype(BF16)
+        for other in range(peers):
+            same_hot[rows, other * LANES : (other + 1) * LANES] = (
+                (column == send_nodes[other]).astype(F32).astype(BF16)
+            )
     build_and_scatter(False)
-    add_returned(diagonal, receive(0))
+    for load in loads[6:]:
+        load.wait()
+    right_shared = pick_shared(right_rows)
+    diag_shared = pick_diagonal()
+    received = receive(0)
+    diag_shared = add_shared(diag_shared, received)
+    send(1, slots(right_shared / diag_shared))
+    add_returned(diagonal, received)
 
     def begin(pair, at, total):
         value = right[:, pl.ds(pl.multiple_of(pair * LANES, LANES), LANES)]
@@ -377,18 +452,24 @@
         return total + value * scaled
 
     sum_rz = over_pairs(begin, zero)
-
-    def apply(source, target, phase):
-        send(phase, pick_shared(source))
-        total = apply_blocks(source, target, False, zero)
+    blocks = pairs // BLOCK
+    edge_blocks = edge_pairs // BLOCK
+    early = edge_blocks + (blocks - edge_blocks) // 2
+
+    def order(phase):
         for p, value in enumerate(receive(phase)):
             ordered[p] = value
-        total = apply_blocks(source, target, True, total)
-        send(phase + 1, gather_ghosts())
-        return total
-
-    sum_zw = apply(z_own, w_own, 1)
-    add_returned(w_own, receive(2))
+
+    sum_zw = apply_blocks(z_own, w_own, edge_blocks, early, zero)
+    order(1)
+    sum_zw = apply_blocks(z_own, w_own, 0, edge_blocks, sum_zw)
+    send(2, gather_ghosts())
+    sum_zw = apply_blocks(z_own, w_own, early, blocks, sum_zw)
+    image_shared = pick_shared(owned_rows(w_own))
+    received = receive(2)
+    image_shared = add_shared(image_shared, received)
+    send(3, slots(image_shared / diag_shared))
+    add_returned(w_own, received)
 
     def middle(pair, at, total):
         value = w_own[at, :]
@@ -397,7 +478,10 @@
         return total + value * scaled
 
     sum_wq = over_pairs(middle, zero)
-    sum_qp = apply(q_own, p_own, 3)
+    sum_qp = apply_blocks(q_own, p_own, edge_blocks, blocks, zero)
+    order(3)
+    sum_qp = apply_blocks(q_own, p_own, 0, edge_blocks, sum_qp)
+    send(4, gather_ghosts())
 
     lane = lax.broadcasted_iota(jnp.int32, (NV, LANES), 1)
     quarter = LANES // 4
@@ -481,6 +565,7 @@
     near_count, far_count = GROUP - 1, devices // GROUP - 1
     vmem = pl.BlockSpec(memory_space=pltpu.VMEM)
     smem = pl.BlockSpec(memory_space=pltpu.SMEM)
+    hbm = pl.BlockSpec(memory_space=pltpu.HBM)
     owned = pltpu.VMEM((pairs * NV, LANES), F32)
     dma = pltpu.SemaphoreType.DMA
     return pl.pallas_call(
@@ -489,13 +574,23 @@
             jax.ShapeDtypeStruct((NV, own_count), F32),
             jax.ShapeDtypeStruct((NV, own_count), F32),
         ),
-        in_specs=[smem, smem] + [vmem] * 9,
+        in_specs=[smem, smem] + [hbm] * 9,
         out_specs=(vmem, vmem),
         scratch_shapes=[
+            pltpu.VMEM((NV, own_count), F32),
+            pltpu.VMEM(stiffness.shape, F32),
+            pltpu.VMEM(mass.shape, F32),
+            pltpu.VMEM((1, elems), jnp.int32),
+            pltpu.VMEM(elem_nodes.shape, jnp.int32),
+            pltpu.VMEM((peers, 1, LANES), jnp.int32),
+            pltpu.VMEM(first.shape, BF16),
+            pltpu.VMEM(second.shape, BF16),
+            pltpu.VMEM(third.shape, BF16),
+            dma((9,)),
             pltpu.VMEM((elems, 3 * LANES), F32),
             pltpu.VMEM((elems, LANES), F32),
             pltpu.VMEM((elems, LANES), jnp.int32),
-            pltpu.VMEM((elems, LANES), jnp.int32),
+            pltpu.VMEM((elems, LANES), F32),
             pltpu.VMEM((pairs, KEYS, 2 * LANES), BF16),
             pltpu.VMEM((elems, LANES), F32),
             owned,
@@ -504,8 +599,9 @@
             owned,
             owned,
             pltpu.VMEM((2 * LANES, live), BF16),
-            pltpu.VMEM((LANES, 2 * live), BF16),
-            pltpu.VMEM((2 * BLOCK * NV, LANES), F32),
+            pltpu.VMEM((live, LANES), BF16),
+            pltpu.VMEM((live, live), BF16),
+            pltpu.VMEM((pairs, LANES), F32),
             pltpu.VMEM((pairs // 2, NV, LANES), F32),
             pltpu.VMEM((5, peers, NV, LANES), F32),
             pltpu.VMEM((5, ways, NV, LANES), F32),
@@ -526,7 +622,7 @@
             dma((far_count,)),
         ],
         compiler_params=pltpu.CompilerParams(
-            collective_id=0, has_side_effects=True, vmem_limit_bytes=48 * 1024 * 1024
+            collective_id=0, has_side_effects=True, vmem_limit_bytes=60 * 1024 * 1024
         ),
     )(
         density,
@@ -536,7 +632,7 @@
         mass,
         region.reshape(1, elems),
         elem_nodes,
-        send_nodes,
+        jnp.transpose(send_nodes, (1, 0, 2)),
         first,
         second,
         third,

time: 66 us -> 53.9 us (0.82)
  local copies, waits for them, and re-layouts: 9.13 us -> 2.72 us
  Pallas kernels: 55.8 us -> 50.4 us
    unnamed x23 -> x4, local copies, waits for them, and re-layouts: 9.13 us -> 2.72 us
    pallas_call x1, Pallas kernels: 55.8 us -> 50.4 us  [on_device(): pl.pallas_call(functools.partial(kernel, devices), out_shape=(jax.ShapeDt...]
where the time goes in v2:
time: 53.9 us; the launch traced here: 53.8 us
  Pallas kernels  50.4 us (94%)
  local copies, waits for them, and re-layouts  2.72 us (5%)
  between operations  0.65 us (1%)
    pallas_call x1, Pallas kernels, on_device(): pl.pallas_call(functools.partial(kernel, devices), out_shape=(jax.ShapeDt...  50.4 us
    unnamed x4, local copies, waits for them, and re-layouts  2.72 us

profile of v2, /device:TPU:1, one launch (start us, length us, event | category | flops | bytes accessed | tf_op | source)
XLA Modules:
  0.0 53.8 jit_solution(15390602295471913688)
XLA Ops:
  0.6 50.4 %shard_map.122 = (f32[8,16384]{1,0:T(8,128)}, f32[8,16384]{1,0:T(8,128)}) custom-call(f32[3]{0:T(128)} %density.1, s32[1,5]{1,0:T(1,128)} %peer_rank.1, f32[8,16384]{1,0:T(8,128)} %right_in.1, f32[3,125,256]{2,1,0:T(8,128)} %stiffness_in.1, f32[125,256]{1,0:T(8,128)} %mass_in.1, s32[1,256]{1,0:T(1,128)} %bitcast.3, s32[125,256]{1,0:T(8,128)} %nodes_in.1, ...), custom_call_target="tpu_custom_call" | custom-call | tf_op jit(solution)/shard_map/pallas_call | solution.py:571
  51.0 0.0 copy-start
  51.0 1.9 %copy.15 = f32[8,16384]{1,0:T(8,128)} copy(f32[8,16384]{1,0:T(8,128)} %get-tuple-element.4) | data formatting | bytes 1048576
  53.0 0.0 copy-done
  53.0 0.8 %copy.16 = f32[8,16384]{1,0:T(8,128)} copy(f32[8,16384]{1,0:T(8,128)S(1)} %copy-done) | data formatting | bytes 1048576
Async XLA Ops:
  51.0 1.9 %copy-start = (f32[8,16384]{1,0:T(8,128)S(1)}, f32[8,16384]{1,0:T(8,128)}, u32[]{:S(2)}) copy-start(f32[8,16384]{1,0:T(8,128)} %get-tuple-element.5) | copy-start | bytes 1572868

commit v3 on v2

--- a/solution.py
+++ b/solution.py
@@ -16,7 +16,7 @@
 LANES = 128
 GROUP = 8
 KEYS = 144
-BLOCK = 16
+BLOCK = 32
 WIDE = 32
 
 
@@ -46,28 +46,58 @@
     return high, low
 
 
+SCALED = np.array(
+    [
+        [-6.09375, 6.8125, -4.875, 1.421875, -0.609375],
+        [-1.703125, 0.0, 3.59375, -0.8671875, 0.35546875],
+        [0.609375, -1.796875, 0.0, 1.796875, -0.609375],
+        [-0.35546875, 0.8671875, -3.59375, 0.0, 1.703125],
+        [0.609375, -1.421875, 4.875, -6.8125, 6.09375],
+    ]
+)
+
+
+def scales():
+    matrix = gll_matrix()
+    equations, logs = [], []
+    for a in range(5):
+        for i in range(5):
+            if a != i or a in (0, 4):
+                equation = np.zeros(10)
+                equation[a] = equation[5 + i] = abs(matrix[a, i])
+                equations.append(equation)
+                logs.append(abs(matrix[a, i]) * np.log(SCALED[a, i] / matrix[a, i]))
+    fitted = np.linalg.lstsq(np.array(equations), np.array(logs), rcond=None)[0]
+    return np.exp(fitted[:5]), np.exp(fitted[5:])
+
+
 def operator_matrices():
-    matrix = gll_matrix().astype(np.float32)
-    eye = np.eye(5, dtype=np.float32)
+    eye = np.eye(5)
 
     def along(small):
-        full = np.zeros((3, LANES, LANES), np.float32)
+        full = np.zeros((3, LANES, LANES))
         full[0, :NPE, :NPE] = np.kron(np.kron(small, eye), eye)
         full[1, :NPE, :NPE] = np.kron(np.kron(eye, small), eye)
         full[2, :NPE, :NPE] = np.kron(np.kron(eye, eye), small)
         return full
 
-    grad = np.concatenate([full.T for full in along(matrix)], axis=1)
-    first_high, first_low = split_numpy(grad)
-    first = np.concatenate([first_high, first_low], axis=1)
+    first = np.concatenate([full.T for full in along(SCALED)], axis=1).astype(jnp.bfloat16)
     first = np.concatenate([first, first], axis=0)
-    back = np.concatenate(list(along(matrix)), axis=0)
-    second = np.concatenate(split_numpy(back), axis=1)
+    second = np.concatenate(list(along(SCALED)), axis=0).astype(jnp.bfloat16)
     second = np.concatenate([second, second], axis=0)
-    square = np.concatenate(list(along(matrix * matrix)), axis=0)
+    square = np.concatenate(list(along(SCALED * SCALED)), axis=0)
     third = np.concatenate(split_numpy(square), axis=1)
     third = np.concatenate([third, third], axis=0)
-    return first, second, third
+    row, column = scales()
+    of_flux = np.zeros((1, 3 * LANES), np.float32)
+    for axis in range(3):
+        factors = [column, column, column]
+        factors[axis] = 1.0 / row
+        product = np.kron(np.kron(factors[0], factors[1]), factors[2])
+        of_flux[0, axis * LANES : axis * LANES + NPE] = product * product
+    of_value = np.zeros((1, LANES), np.float32)
+    of_value[0, :NPE] = 1.0 / np.kron(np.kron(column, column), column)
+    return first, second, third, of_flux, of_value
 
 
 def split(value):
@@ -104,6 +134,8 @@
     first_in,
     second_in,
     third_in,
+    of_flux,
+    of_value,
     solution_out,
     residual_out,
     right,
@@ -121,6 +153,8 @@
     node_table,
     key_table,
     hot,
+    ghost_hot,
+    results,
     diag_term,
     diagonal,
     z_own,
@@ -151,6 +185,10 @@
     far_recv,
 ):
     me = lax.axis_index("dom")
+
+    def tile(pair):
+        return slice(None), pl.ds(pl.multiple_of(pair * LANES, LANES), LANES)
+
     incoming = [incoming_0, incoming_1, incoming_2, incoming_3, incoming_4]
     elems = nodes.shape[1]
     pairs = elems // 2
@@ -179,39 +217,46 @@
     for other in candidates + near + far:
         pl.semaphore_signal(barrier, inc=1, device_id=(other,), device_id_type=MESH)
 
-    node_table[...] = jnp.zeros_like(node_table)
-    loads[0].wait()
-    halves = [slice(half * LANES, (half + 1) * LANES) for half in range(elems // LANES)]
-    for columns in halves:
+    own_count = pairs * LANES
+    value_scale = of_value[...]
+
+    def tables(half):
+        columns = slice(half * LANES, (half + 1) * LANES)
+        node_table[columns] = jnp.zeros((LANES, LANES), jnp.int32)
         node_table[columns, :NPE] = nodes[:, columns].T
-    table = node_table[...]
-    own_count = pairs * LANES
-    pair_of = lax.broadcasted_iota(jnp.int32, table.shape, 0) // 2
-    key = jnp.where(
-        table < own_count, table & (LANES - 1), LANES + ((table - run * pair_of) & (LANES - 1))
-    )
-    key_table[...] = jnp.where(
-        lax.broadcasted_iota(jnp.int32, table.shape, 1) < NPE, key, 255
-    ).astype(F32)
-    stiff[...] = jnp.zeros_like(stiff)
-    mass_term[...] = jnp.zeros_like(mass_term)
-    for load in loads[1:6]:
-        load.wait()
-    for columns in halves:
+        table = node_table[columns]
+        pair_of = half * (LANES // 2) + lax.broadcasted_iota(jnp.int32, table.shape, 0) // 2
+        key = jnp.where(
+            table < own_count, table & (LANES - 1), LANES + ((table - run * pair_of) & (LANES - 1))
+        )
+        key_table[columns] = jnp.where(
+            lax.broadcasted_iota(jnp.int32, table.shape, 1) < NPE, key, 255
+        ).astype(F32)
+        stiff[columns] = jnp.zeros((LANES, 3 * LANES), F32)
+        mass_term[columns] = jnp.zeros((LANES, LANES), F32)
         for axis in range(3):
-            stiff[columns, axis * LANES : axis * LANES + NPE] = stiffness[axis, :, columns].T
+            at = slice(axis * LANES, axis * LANES + NPE)
+            stiff[columns, at] = stiffness[axis, :, columns].T * of_flux[:, at]
         tag = region[:, columns]
         weight = jnp.where(tag == 0, density[0], jnp.where(tag == 1, density[1], density[2]))
         mass_term[columns, :NPE] = (mass[:, columns] * weight).T
+        diag_out = matmul(parts(stiff[columns]), third[...])
+        diag_term[columns] = (diag_out[:, :LANES] + diag_out[:, LANES:]) * (
+            value_scale * value_scale
+        ) + mass_term[columns]
+
     ghost[...] = jnp.zeros_like(ghost)
-
-    diag_out = matmul(parts(stiff[...]), third[...])
-    diag_term[...] = diag_out[:, :LANES] + diag_out[:, LANES:] + mass_term[...]
-
-    def scatter_pair(pair, both, count):
+    for load in loads[:6]:
+        load.wait()
+    tables(0)
+
+    def scatter_rows(both, where):
         rows = jnp.concatenate([both, both - both.astype(BF16).astype(F32)], axis=0).astype(BF16)
-        summed = matmul_nt(rows, hot[pair, :count])
+        summed = matmul_nt(rows, where)
         return summed[:NV] + summed[NV:]
+
+    def scatter_pair(pair, both):
+        return scatter_rows(both, hot[pair])
 
     def gather_ghosts():
         sums = [jnp.zeros((NV, LANES), F32) for _ in range(peers)]
@@ -283,16 +328,19 @@
                 found = window == number
                 high_rows.append(jnp.where(found, high, none))
                 low_rows.append(jnp.where(found, low, none))
-            at = pl.ds(pl.multiple_of(block * WIDE * NV, WIDE * NV), WIDE * NV)
             summed = matmul(jnp.concatenate(high_rows + low_rows, axis=0), back_hot[...])
-            own[at, :] = own[at, :] + (summed[: WIDE * NV] + summed[WIDE * NV :])
+            summed = summed[: WIDE * NV] + summed[WIDE * NV :]
+            for i in range(WIDE):
+                at = tile(block * WIDE + i)
+                own[at] = own[at] + summed[i * NV : (i + 1) * NV]
             return carry
 
         lax.fori_loop(0, pairs // WIDE, body, 0)
 
-    def pick_shared(load):
+    def pick_shared(own):
         def body(block, total):
-            spread = matmul(parts(load(block)), lane_hot[...])
+            rows = jnp.concatenate([own[tile(block * WIDE + i)] for i in range(WIDE)], axis=0)
+            spread = matmul(parts(rows), lane_hot[...])
             for i in range(WIDE):
                 total = total + jnp.where(
                     send_window == block * WIDE + i, spread[i * NV : (i + 1) * NV], 0.0
@@ -301,22 +349,6 @@
 
         return lax.fori_loop(0, pairs // WIDE, body, jnp.zeros((NV, live), F32))
 
-    def owned_rows(own):
-        def load(block):
-            return own[pl.ds(pl.multiple_of(block * WIDE * NV, WIDE * NV), WIDE * NV), :]
-
-        return load
-
-    def right_rows(block):
-        base = block * WIDE * LANES
-        return jnp.concatenate(
-            [
-                right[:, pl.ds(pl.multiple_of(base + i * LANES, LANES), LANES)]
-                for i in range(WIDE)
-            ],
-            axis=0,
-        )
-
     def pick_diagonal():
         spread = matmul(parts(diag_rows[...]), lane_hot[...])
         number = lax.broadcasted_iota(jnp.int32, (pairs, live), 0)
@@ -332,29 +364,43 @@
     def slots(value):
         return [value[:, p * LANES : (p + 1) * LANES] for p in range(peers)]
 
-    def build_and_scatter(edge):
-        count = KEYS if edge else LANES
-        row_of = lax.broadcasted_iota(jnp.int32, (16, 2 * LANES), 0)
-        one, none = jnp.ones((16, 2 * LANES), BF16), jnp.zeros((16, 2 * LANES), BF16)
-
-        def body(index, carry):
-            pair = index if edge else index + edge_pairs
-            both = pl.ds(2 * pair, 1), pl.ds(2 * pair + 1, 1)
-            keys = jnp.concatenate([key_table[both[0], :], key_table[both[1], :]], axis=1)
-            keys = jnp.broadcast_to(keys, (16, 2 * LANES)).astype(BF16)
-            for tile in range(count // 16):
-                number = (row_of + 16 * tile).astype(F32).astype(BF16)
-                hot[pair, 16 * tile : 16 * tile + 16] = jnp.where(keys == number, one, none)
-            term = jnp.concatenate([diag_term[both[0], :], diag_term[both[1], :]], axis=1)
-            summed = scatter_pair(pair, jnp.broadcast_to(term, (NV, 2 * LANES)), count)
-            at = pl.ds(pl.multiple_of(pair * NV, NV), NV)
-            diagonal[at, :] = summed[:, :LANES]
-            diag_rows[pl.ds(pair, 1), :] = summed[:1, :LANES]
-            if edge:
-                ghost[pair, :, : KEYS - LANES] = summed[:, LANES:]
+    row_of = lax.broadcasted_iota(jnp.int32, (16, 2 * LANES), 0)
+    one, none = jnp.ones((16, 2 * LANES), BF16), jnp.zeros((16, 2 * LANES), BF16)
+
+    def keys_of(pair):
+        both = pl.ds(2 * pair, 1), pl.ds(2 * pair + 1, 1)
+        keys = jnp.concatenate([key_table[both[0], :], key_table[both[1], :]], axis=1)
+        return jnp.broadcast_to(keys, (16, 2 * LANES)).astype(BF16)
+
+    def diag_of(pair):
+        both = pl.ds(2 * pair, 1), pl.ds(2 * pair + 1, 1)
+        term = jnp.concatenate([diag_term[both[0], :], diag_term[both[1], :]], axis=1)
+        return jnp.broadcast_to(term, (NV, 2 * LANES))
+
+    def strip(keys, begin):
+        number = (row_of + begin).astype(F32).astype(BF16)
+        return jnp.where(keys == number, one, none)
+
+    def build_ghosts():
+        def body(pair, carry):
+            where = strip(keys_of(pair), LANES)
+            ghost_hot[pair] = where
+            ghost[pair, :, : KEYS - LANES] = scatter_rows(diag_of(pair), where)
             return carry
 
-        lax.fori_loop(0, edge_pairs, body, 0, unroll=4)
+        lax.fori_loop(0, edge_pairs, body, 0, unroll=8)
+
+    def build_owned():
+        def body(pair, carry):
+            keys = keys_of(pair)
+            for begin in range(0, LANES, 16):
+                hot[pair, begin : begin + 16] = strip(keys, begin)
+            summed = scatter_pair(pair, diag_of(pair))
+            diagonal[tile(pair)] = summed
+            diag_rows[pl.ds(pair, 1), :] = summed[:1]
+            return carry
+
+        lax.fori_loop(0, pairs, body, 0, unroll=4)
 
     def apply_blocks(source, target, begin_block, end_block, total):
         edge = begin_block < edge_pairs // BLOCK
@@ -363,7 +409,7 @@
             gathered = []
             for i in range(BLOCK):
                 pair = block * BLOCK + i
-                own = source[pl.ds(pl.multiple_of(pair * NV, NV), NV), :]
+                own = source[tile(pair)]
                 if edge:
                     base = pair * run
                     lane = lax.broadcasted_iota(jnp.int32, (NV, LANES), 1)
@@ -382,8 +428,7 @@
                         picked = jnp.where(node < own_count, picked, remote_value)
                     gathered.append(picked)
             value = jnp.concatenate(gathered, axis=0)
-            grad = matmul(parts(value), first[...])
-            flux = grad[:, : 3 * LANES] + grad[:, 3 * LANES :]
+            flux = matmul(parts(value * value_scale), first[...])
             scaled = []
             masses = []
             for i in range(2 * BLOCK):
@@ -391,7 +436,7 @@
                 scaled.append(flux[i * NV : (i + 1) * NV] * stiff[at, :])
                 masses.append(jnp.broadcast_to(mass_term[at, :], (NV, LANES)))
             back = matmul(parts(jnp.concatenate(scaled, axis=0)), second[...])
-            result = back[:, :LANES] + back[:, LANES:] + jnp.concatenate(masses, axis=0) * value
+            result = back * value_scale + jnp.concatenate(masses, axis=0) * value
             product = value * result
             for i in range(2 * BLOCK):
                 total = total + product[i * NV : (i + 1) * NV]
@@ -401,22 +446,30 @@
                 both = jnp.concatenate(
                     [result[low : low + NV], result[low + NV : low + 2 * NV]], axis=1
                 )
-                summed = scatter_pair(pair, both, KEYS if edge else LANES)
-                target[pl.ds(pl.multiple_of(pair * NV, NV), NV), :] = summed[:, :LANES]
                 if edge:
-                    ghost[pair, :, : KEYS - LANES] = summed[:, LANES:]
+                    results[pair] = both
+                    ghost[pair, :, : KEYS - LANES] = scatter_rows(both, ghost_hot[pair])
+                else:
+                    target[tile(pair)] = scatter_pair(pair, both)
             return total
 
         return lax.fori_loop(begin_block, end_block, body, total)
+
+    def place_edge(target):
+        def body(pair, carry):
+            target[tile(pair)] = scatter_pair(pair, results[pair])
+            return carry
+
+        lax.fori_loop(0, edge_pairs, body, 0, unroll=8)
 
     def over_pairs(step, total):
         def body(pair, total):
-            return step(pair, pl.ds(pl.multiple_of(pair * NV, NV), NV), total)
+            return step(tile(pair), total)
 
         return lax.fori_loop(0, pairs, body, total, unroll=8)
 
     zero = jnp.zeros((NV, LANES), F32)
-    build_and_scatter(True)
+    build_ghosts()
     pl.semaphore_wait(barrier, len(candidates) + len(near) + len(far))
     send(0, gather_ghosts())
 
@@ -435,20 +488,21 @@
             same_hot[rows, other * LANES : (other + 1) * LANES] = (
                 (column == send_nodes[other]).astype(F32).astype(BF16)
             )
-    build_and_scatter(False)
+    tables(1)
+    build_owned()
     for load in loads[6:]:
         load.wait()
-    right_shared = pick_shared(right_rows)
+    right_shared = pick_shared(right)
     diag_shared = pick_diagonal()
     received = receive(0)
     diag_shared = add_shared(diag_shared, received)
     send(1, slots(right_shared / diag_shared))
     add_returned(diagonal, received)
 
-    def begin(pair, at, total):
-        value = right[:, pl.ds(pl.multiple_of(pair * LANES, LANES), LANES)]
-        scaled = value / diagonal[at, :]
-        z_own[at, :] = scaled
+    def begin(at, total):
+        value = right[at]
+        scaled = value / diagonal[at]
+        z_own[at] = scaled
         return total + value * scaled
 
     sum_rz = over_pairs(begin, zero)
@@ -464,17 +518,18 @@
     order(1)
     sum_zw = apply_blocks(z_own, w_own, 0, edge_blocks, sum_zw)
     send(2, gather_ghosts())
+    place_edge(w_own)
     sum_zw = apply_blocks(z_own, w_own, early, blocks, sum_zw)
-    image_shared = pick_shared(owned_rows(w_own))
+    image_shared = pick_shared(w_own)
     received = receive(2)
     image_shared = add_shared(image_shared, received)
     send(3, slots(image_shared / diag_shared))
     add_returned(w_own, received)
 
-    def middle(pair, at, total):
-        value = w_own[at, :]
-        scaled = value / diagonal[at, :]
-        q_own[at, :] = scaled
+    def middle(at, total):
+        value = w_own[at]
+        scaled = value / diagonal[at]
+        q_own[at] = scaled
         return total + value * scaled
 
     sum_wq = over_pairs(middle, zero)
@@ -514,6 +569,7 @@
     partial[0] = packed
     for step in range(len(near)):
         near_copy(step).start()
+    place_edge(p_own)
     for step in range(len(near)):
         near_copy(step).wait_recv()
         packed = packed + near_in[step]
@@ -537,10 +593,9 @@
     outer = jnp.broadcast_to(alpha + second_alpha * ratio, (NV, LANES))
     inner = jnp.broadcast_to(alpha * second_alpha, (NV, LANES))
 
-    def finish(pair, at, total):
-        out = pl.ds(pl.multiple_of(pair * LANES, LANES), LANES)
-        solution_out[:, out] = outer * z_own[at, :] - inner * q_own[at, :]
-        residual_out[:, out] = right[:, out] - outer * w_own[at, :] + inner * p_own[at, :]
+    def finish(at, total):
+        solution_out[at] = outer * z_own[at] - inner * q_own[at]
+        residual_out[at] = right[at] - outer * w_own[at] + inner * p_own[at]
         return total
 
     over_pairs(finish, zero)
@@ -554,7 +609,9 @@
 
 
 def on_device(devices, right, stiffness, mass, region, density, elem_nodes, peer_rank, send_nodes):
-    first, second, third = (jnp.asarray(matrix) for matrix in operator_matrices())
+    first, second, third, of_flux, of_value = (
+        jnp.asarray(matrix) for matrix in operator_matrices()
+    )
     own_count = right.shape[1]
     elems = elem_nodes.shape[1]
     pairs = elems // 2
@@ -566,15 +623,12 @@
     vmem = pl.BlockSpec(memory_space=pltpu.VMEM)
     smem = pl.BlockSpec(memory_space=pltpu.SMEM)
     hbm = pl.BlockSpec(memory_space=pltpu.HBM)
-    owned = pltpu.VMEM((pairs * NV, LANES), F32)
+    owned = pltpu.VMEM((NV, own_count), F32)
     dma = pltpu.SemaphoreType.DMA
     return pl.pallas_call(
         functools.partial(kernel, devices),
-        out_shape=(
-            jax.ShapeDtypeStruct((NV, own_count), F32),
-            jax.ShapeDtypeStruct((NV, own_count), F32),
-        ),
-        in_specs=[smem, smem] + [hbm] * 9,
+        out_shape=(jax.ShapeDtypeStruct((NV, own_count), F32),) * 2,
+        in_specs=[smem, smem] + [hbm] * 9 + [vmem] * 2,
         out_specs=(vmem, vmem),
         scratch_shapes=[
             pltpu.VMEM((NV, own_count), F32),
@@ -591,7 +645,9 @@
             pltpu.VMEM((elems, LANES), F32),
             pltpu.VMEM((elems, LANES), jnp.int32),
             pltpu.VMEM((elems, LANES), F32),
-            pltpu.VMEM((pairs, KEYS, 2 * LANES), BF16),
+            pltpu.VMEM((pairs, LANES, 2 * LANES), BF16),
+            pltpu.VMEM((pairs // 2, KEYS - LANES, 2 * LANES), BF16),
+            pltpu.VMEM((pairs // 2, NV, 2 * LANES), F32),
             pltpu.VMEM((elems, LANES), F32),
             owned,
             owned,
@@ -636,6 +692,8 @@
         first,
         second,
         third,
+        of_flux,
+        of_value,
     )
 
 

time: 53.9 us -> 51 us (0.946)
  Pallas kernels: 50.4 us -> 47.5 us
    pallas_call x1, Pallas kernels: 50.4 us -> 47.5 us  [on_device(): pl.pallas_call(functools.partial(kernel, devices), out_shape=(jax.ShapeDt...]
where the time goes in v3:
time: 51 us; the launch traced here: 50.8 us
  Pallas kernels  47.5 us (93%)
  local copies, waits for them, and re-layouts  2.72 us (5%)
  between operations  0.65 us (1%)
    pallas_call x1, Pallas kernels, on_device(): pl.pallas_call(functools.partial(kernel, devices), out_shape=(jax.ShapeDt...  47.5 us
    unnamed x4, local copies, waits for them, and re-layouts  2.72 us

profile of v3, /device:TPU:1, one launch (start us, length us, event | category | flops | bytes accessed | tf_op | source)
XLA Modules:
  0.0 50.8 jit_solution(16448064965139885053)
XLA Ops:
  0.6 47.5 %shard_map.140 = (f32[8,16384]{1,0:T(8,128)}, f32[8,16384]{1,0:T(8,128)}) custom-call(f32[3]{0:T(128)} %density.1, s32[1,5]{1,0:T(1,128)} %peer_rank.1, f32[8,16384]{1,0:T(8,128)} %right_in.1, f32[3,125,256]{2,1,0:T(8,128)} %stiffness_in.1, f32[125,256]{1,0:T(8,128)} %mass_in.1, s32[1,256]{1,0:T(1,128)} %bitcast.3, s32[125,256]{1,0:T(8,128)} %nodes_in.1, ...), custom_call_target="tpu_custom_call" | custom-call | tf_op jit(solution)/shard_map/pallas_call | solution.py:628
  48.1 0.0 copy-start
  48.1 1.9 %copy.17 = f32[8,16384]{1,0:T(8,128)} copy(f32[8,16384]{1,0:T(8,128)} %get-tuple-element.4) | data formatting | bytes 1048576
  50.0 0.0 copy-done
  50.1 0.8 %copy.18 = f32[8,16384]{1,0:T(8,128)} copy(f32[8,16384]{1,0:T(8,128)S(1)} %copy-done) | data formatting | bytes 1048576
Async XLA Ops:
  48.1 1.9 %copy-start = (f32[8,16384]{1,0:T(8,128)S(1)}, f32[8,16384]{1,0:T(8,128)}, u32[]{:S(2)}) copy-start(f32[8,16384]{1,0:T(8,128)} %get-tuple-element.5) | copy-start | bytes 1572868

commit v4 on v3

--- a/solution.py
+++ b/solution.py
@@ -18,6 +18,7 @@
 KEYS = 144
 BLOCK = 32
 WIDE = 32
+PICK = 64
 
 
 def gll_matrix():
@@ -173,7 +174,8 @@
     incoming_2,
     incoming_3,
     incoming_4,
-    ordered,
+    aligned,
+    edge_values,
     send_sem,
     recv_sem,
     partial,
@@ -204,8 +206,8 @@
     near = [me - me % GROUP + (me + step) % GROUP for step in range(1, GROUP)]
     far = [(me + step * GROUP) % devices for step in range(1, far_count)]
 
-    sources = [nodes_in, send_in, stiffness_in, region_in, mass_in, third_in, right_in, first_in, second_in]
-    places = [nodes, send_nodes, stiffness, region, mass, third, right, first, second]
+    sources = [send_in, nodes_in, stiffness_in, region_in, mass_in, third_in, right_in, first_in, second_in]
+    places = [send_nodes, nodes, stiffness, region, mass, third, right, first, second]
     loads = [
         pltpu.make_async_copy(source, place, in_sem.at[index])
         for index, (source, place) in enumerate(zip(sources, places))
@@ -217,6 +219,22 @@
     for other in candidates + near + far:
         pl.semaphore_signal(barrier, inc=1, device_id=(other,), device_id_type=MESH)
 
+    loads[0].wait()
+    send_row = jnp.concatenate([send_nodes[p] for p in range(peers)], axis=1)
+    send_window = jnp.broadcast_to(send_row // LANES, (NV, live))
+    lane_number = lax.broadcasted_iota(jnp.int32, (LANES, live), 0)
+    picks = (lane_number == (send_row & (LANES - 1))).astype(F32).astype(BF16)
+    lane_hot[:LANES] = picks
+    lane_hot[LANES:] = picks
+    lane_number = lax.broadcasted_iota(jnp.int32, (LANES, LANES), 1)
+    for p in range(peers):
+        column = jnp.broadcast_to(send_nodes[p], (LANES, LANES)).T
+        rows = slice(p * LANES, (p + 1) * LANES)
+        back_hot[rows] = (lane_number == (column & (LANES - 1))).astype(F32).astype(BF16)
+        for other in range(peers):
+            same_hot[rows, other * LANES : (other + 1) * LANES] = (
+                (column == send_nodes[other]).astype(F32).astype(BF16)
+            )
     own_count = pairs * LANES
     value_scale = of_value[...]
 
@@ -246,7 +264,7 @@
         ) + mass_term[columns]
 
     ghost[...] = jnp.zeros_like(ghost)
-    for load in loads[:6]:
+    for load in loads[1:6]:
         load.wait()
     tables(0)
 
@@ -339,15 +357,15 @@
 
     def pick_shared(own):
         def body(block, total):
-            rows = jnp.concatenate([own[tile(block * WIDE + i)] for i in range(WIDE)], axis=0)
+            rows = jnp.concatenate([own[tile(block * PICK + i)] for i in range(PICK)], axis=0)
             spread = matmul(parts(rows), lane_hot[...])
-            for i in range(WIDE):
+            for i in range(PICK):
                 total = total + jnp.where(
-                    send_window == block * WIDE + i, spread[i * NV : (i + 1) * NV], 0.0
+                    send_window == block * PICK + i, spread[i * NV : (i + 1) * NV], 0.0
                 )
             return total
 
-        return lax.fori_loop(0, pairs // WIDE, body, jnp.zeros((NV, live), F32))
+        return lax.fori_loop(0, pairs // PICK, body, jnp.zeros((NV, live), F32))
 
     def pick_diagonal():
         spread = matmul(parts(diag_rows[...]), lane_hot[...])
@@ -402,6 +420,24 @@
 
         lax.fori_loop(0, pairs, body, 0, unroll=4)
 
+    def gather_pair(source, pair):
+        own = source[tile(pair)]
+        gathered = []
+        for side in range(2):
+            node = jnp.broadcast_to(node_table[pl.ds(2 * pair + side, 1), :], (NV, LANES))
+            picked = jnp.take_along_axis(
+                own, node & (LANES - 1), axis=1, mode="promise_in_bounds"
+            )
+            gathered.append(jnp.where(node < own_count, picked, 0.0))
+        return gathered
+
+    def gather_edge(source):
+        def body(pair, carry):
+            edge_values[pair] = jnp.concatenate(gather_pair(source, pair), axis=0)
+            return carry
+
+        lax.fori_loop(0, edge_pairs, body, 0, unroll=16)
+
     def apply_blocks(source, target, begin_block, end_block, total):
         edge = begin_block < edge_pairs // BLOCK
 
@@ -409,24 +445,13 @@
             gathered = []
             for i in range(BLOCK):
                 pair = block * BLOCK + i
-                own = source[tile(pair)]
                 if edge:
-                    base = pair * run
-                    lane = lax.broadcasted_iota(jnp.int32, (NV, LANES), 1)
-                    begin = base % LANES
-                    received = jnp.where(
-                        lane >= begin, ordered[base // LANES], ordered[(base + run - 1) // LANES]
-                    )
-                for side in range(2):
-                    node = jnp.broadcast_to(node_table[pl.ds(2 * pair + side, 1), :], (NV, LANES))
-                    lanes = node & (LANES - 1)
-                    picked = jnp.take_along_axis(own, lanes, axis=1, mode="promise_in_bounds")
-                    if edge:
-                        remote_value = jnp.take_along_axis(
-                            received, lanes, axis=1, mode="promise_in_bounds"
-                        )
-                        picked = jnp.where(node < own_count, picked, remote_value)
-                    gathered.append(picked)
+                    spread = matmul(aligned[pair][:, : KEYS - LANES], ghost_hot[pair])
+                    spread = spread[:NV] + spread[NV:]
+                    gathered.append(edge_values[pair, :NV] + spread[:, :LANES])
+                    gathered.append(edge_values[pair, NV:] + spread[:, LANES:])
+                else:
+                    gathered += gather_pair(source, pair)
             value = jnp.concatenate(gathered, axis=0)
             flux = matmul(parts(value * value_scale), first[...])
             scaled = []
@@ -473,21 +498,6 @@
     pl.semaphore_wait(barrier, len(candidates) + len(near) + len(far))
     send(0, gather_ghosts())
 
-    send_row = jnp.concatenate([send_nodes[p] for p in range(peers)], axis=1)
-    send_window = jnp.broadcast_to(send_row // LANES, (NV, live))
-    lane_number = lax.broadcasted_iota(jnp.int32, (LANES, live), 0)
-    picks = (lane_number == (send_row & (LANES - 1))).astype(F32).astype(BF16)
-    lane_hot[:LANES] = picks
-    lane_hot[LANES:] = picks
-    lane_number = lax.broadcasted_iota(jnp.int32, (LANES, LANES), 1)
-    for p in range(peers):
-        column = jnp.broadcast_to(send_nodes[p], (LANES, LANES)).T
-        rows = slice(p * LANES, (p + 1) * LANES)
-        back_hot[rows] = (lane_number == (column & (LANES - 1))).astype(F32).astype(BF16)
-        for other in range(peers):
-            same_hot[rows, other * LANES : (other + 1) * LANES] = (
-                (column == send_nodes[other]).astype(F32).astype(BF16)
-            )
     tables(1)
     build_owned()
     for load in loads[6:]:
@@ -511,9 +521,21 @@
     early = edge_blocks + (blocks - edge_blocks) // 2
 
     def order(phase):
-        for p, value in enumerate(receive(phase)):
-            ordered[p] = value
-
+        received = receive(phase)
+        lane = lax.broadcasted_iota(jnp.int32, (NV, LANES), 1)
+        for pair in range(edge_pairs):
+            start = pair * run % LANES
+            here, last = pair * run // LANES, (pair * run + run - 1) // LANES
+            row = received[here]
+            if here != last:
+                row = jnp.where(lane >= start, row, received[last])
+            if start:
+                row = pltpu.roll(row, LANES - start, 1)
+            aligned[pair] = jnp.concatenate(
+                [row, row - row.astype(BF16).astype(F32)], axis=0
+            ).astype(BF16)
+
+    gather_edge(z_own)
     sum_zw = apply_blocks(z_own, w_own, edge_blocks, early, zero)
     order(1)
     sum_zw = apply_blocks(z_own, w_own, 0, edge_blocks, sum_zw)
@@ -533,6 +555,7 @@
         return total + value * scaled
 
     sum_wq = over_pairs(middle, zero)
+    gather_edge(q_own)
     sum_qp = apply_blocks(q_own, p_own, edge_blocks, blocks, zero)
     order(3)
     sum_qp = apply_blocks(q_own, p_own, 0, edge_blocks, sum_qp)
@@ -666,7 +689,8 @@
             pltpu.VMEM((ways, NV, LANES), F32),
             pltpu.VMEM((ways, NV, LANES), F32),
             pltpu.VMEM((ways, NV, LANES), F32),
-            pltpu.VMEM((peers, NV, LANES), F32),
+            pltpu.VMEM((pairs // 2, 2 * NV, LANES), BF16),
+            pltpu.VMEM((pairs // 2, 2 * NV, LANES), F32),
             dma((5, ways)),
             dma((5, ways)),
             pltpu.VMEM((2, NV, LANES), F32),

time: 51 us -> 50.3 us (0.986)
  Pallas kernels: 47.5 us -> 46.8 us
    pallas_call x1, Pallas kernels: 47.5 us -> 46.8 us  [on_device(): pl.pallas_call(functools.partial(kernel, devices), out_shape=(jax.ShapeDt...]
where the time goes in v4:
time: 50.3 us; the launch traced here: 50.1 us
  Pallas kernels  46.8 us (93%)
  local copies, waits for them, and re-layouts  2.72 us (5%)
  between operations  0.65 us (1%)
    pallas_call x1, Pallas kernels, on_device(): pl.pallas_call(functools.partial(kernel, devices), out_shape=(jax.ShapeDt...  46.8 us
    unnamed x4, local copies, waits for them, and re-layouts  2.72 us

profile of v4, /device:TPU:1, one launch (start us, length us, event | category | flops | bytes accessed | tf_op | source)
XLA Modules:
  0.0 50.1 jit_solution(5336583647313133415)
XLA Ops:
  0.6 46.8 %shard_map.140 = (f32[8,16384]{1,0:T(8,128)}, f32[8,16384]{1,0:T(8,128)}) custom-call(f32[3]{0:T(128)} %density.1, s32[1,5]{1,0:T(1,128)} %peer_rank.1, f32[8,16384]{1,0:T(8,128)} %right_in.1, f32[3,125,256]{2,1,0:T(8,128)} %stiffness_in.1, f32[125,256]{1,0:T(8,128)} %mass_in.1, s32[1,256]{1,0:T(1,128)} %bitcast.3, s32[125,256]{1,0:T(8,128)} %nodes_in.1, ...), custom_call_target="tpu_custom_call" | custom-call | tf_op jit(solution)/shard_map/pallas_call | solution.py:651
  47.4 0.0 copy-start
  47.4 1.9 %copy.17 = f32[8,16384]{1,0:T(8,128)} copy(f32[8,16384]{1,0:T(8,128)} %get-tuple-element.4) | data formatting | bytes 1048576
  49.3 0.0 copy-done
  49.3 0.8 %copy.18 = f32[8,16384]{1,0:T(8,128)} copy(f32[8,16384]{1,0:T(8,128)S(1)} %copy-done) | data formatting | bytes 1048576
Async XLA Ops:
  47.4 1.9 %copy-start = (f32[8,16384]{1,0:T(8,128)S(1)}, f32[8,16384]{1,0:T(8,128)}, u32[]{:S(2)}) copy-start(f32[8,16384]{1,0:T(8,128)} %get-tuple-element.5) | copy-start | bytes 1572868

commit v5 on v4

--- a/solution.py
+++ b/solution.py
@@ -176,6 +176,7 @@
     incoming_4,
     aligned,
     edge_values,
+    flux_parts,
     send_sem,
     recv_sem,
     partial,
@@ -480,6 +481,56 @@
 
         return lax.fori_loop(begin_block, end_block, body, total)
 
+    def edge_energy(total):
+        def body(block, total):
+            gathered, scaled = [], []
+            for i in range(BLOCK):
+                pair = block * BLOCK + i
+                spread = matmul(aligned[pair][:, : KEYS - LANES], ghost_hot[pair])
+                spread = spread[:NV] + spread[NV:]
+                spread = jnp.concatenate([spread[:, :LANES], spread[:, LANES:]], axis=0)
+                value = edge_values[pair] + spread
+                edge_values[pair] = value
+                gathered.append(value)
+            value = jnp.concatenate(gathered, axis=0)
+            flux = matmul(parts(value * value_scale), first[...])
+            for i in range(2 * BLOCK):
+                at = pl.ds(block * 2 * BLOCK + i, 1)
+                low, high = i * NV, (i + 1) * NV
+                scaled.append(flux[low:high] * stiff[at, :])
+                product = scaled[-1] * flux[low:high]
+                total = total + (product[:, :LANES] + product[:, LANES : 2 * LANES])
+                total = total + product[:, 2 * LANES :]
+                total = total + mass_term[at, :] * (value[low:high] * value[low:high])
+            rows = 2 * BLOCK * NV
+            at = pl.ds(pl.multiple_of(block * rows, rows), rows)
+            flux_parts[at, :] = parts(jnp.concatenate(scaled, axis=0))
+            return total
+
+        return lax.fori_loop(0, edge_pairs // BLOCK, body, total)
+
+    def edge_results():
+        def body(block, carry):
+            rows = 2 * BLOCK * NV
+            at = pl.ds(pl.multiple_of(block * rows, rows), rows)
+            back = matmul(flux_parts[at, :], second[...]) * value_scale
+            for i in range(BLOCK):
+                pair = block * BLOCK + i
+                sides = []
+                for side in range(2):
+                    low = (2 * i + side) * NV
+                    sides.append(
+                        back[low : low + NV]
+                        + mass_term[pl.ds(2 * pair + side, 1), :]
+                        * edge_values[pair, side * NV : (side + 1) * NV]
+                    )
+                both = jnp.concatenate(sides, axis=1)
+                results[pair] = both
+                ghost[pair, :, : KEYS - LANES] = scatter_rows(both, ghost_hot[pair])
+            return carry
+
+        lax.fori_loop(0, edge_pairs // BLOCK, body, 0)
+
     def place_edge(target):
         def body(pair, carry):
             target[tile(pair)] = scatter_pair(pair, results[pair])
@@ -558,8 +609,7 @@
     gather_edge(q_own)
     sum_qp = apply_blocks(q_own, p_own, edge_blocks, blocks, zero)
     order(3)
-    sum_qp = apply_blocks(q_own, p_own, 0, edge_blocks, sum_qp)
-    send(4, gather_ghosts())
+    sum_qp = edge_energy(sum_qp)
 
     lane = lax.broadcasted_iota(jnp.int32, (NV, LANES), 1)
     quarter = LANES // 4
@@ -592,6 +642,8 @@
     partial[0] = packed
     for step in range(len(near)):
         near_copy(step).start()
+    edge_results()
+    send(4, gather_ghosts())
     place_edge(p_own)
     for step in range(len(near)):
         near_copy(step).wait_recv()
@@ -691,6 +743,7 @@
             pltpu.VMEM((ways, NV, LANES), F32),
             pltpu.VMEM((pairs // 2, 2 * NV, LANES), BF16),
             pltpu.VMEM((pairs // 2, 2 * NV, LANES), F32),
+            pltpu.VMEM((pairs * NV, 6 * LANES), BF16),
             dma((5, ways)),
             dma((5, ways)),
             pltpu.VMEM((2, NV, LANES), F32),

time: 50.3 us -> 49.5 us (0.984)
  Pallas kernels: 46.8 us -> 45.8 us
    pallas_call x1, Pallas kernels: 46.8 us -> 45.8 us  [on_device(): pl.pallas_call(functools.partial(kernel, devices), out_shape=(jax.ShapeDt...]
where the time goes in v5:
time: 49.5 us; the launch traced here: 49.2 us
  Pallas kernels  45.8 us (93%)
  local copies, waits for them, and re-layouts  2.72 us (5%)
  between operations  0.65 us (1%)
    pallas_call x1, Pallas kernels, on_device(): pl.pallas_call(functools.partial(kernel, devices), out_shape=(jax.ShapeDt...  45.8 us
    unnamed x4, local copies, waits for them, and re-layouts  2.72 us

profile of v5, /device:TPU:1, one launch (start us, length us, event | category | flops | bytes accessed | tf_op | source)
XLA Modules:
  0.0 49.2 jit_solution(15486969448473748062)
XLA Ops:
  0.6 45.8 %shard_map.140 = (f32[8,16384]{1,0:T(8,128)}, f32[8,16384]{1,0:T(8,128)}) custom-call(f32[3]{0:T(128)} %density.1, s32[1,5]{1,0:T(1,128)} %peer_rank.1, f32[8,16384]{1,0:T(8,128)} %right_in.1, f32[3,125,256]{2,1,0:T(8,128)} %stiffness_in.1, f32[125,256]{1,0:T(8,128)} %mass_in.1, s32[1,256]{1,0:T(1,128)} %bitcast.3, s32[125,256]{1,0:T(8,128)} %nodes_in.1, ...), custom_call_target="tpu_custom_call" | custom-call | tf_op jit(solution)/shard_map/pallas_call | solution.py:703
  46.4 0.0 copy-start
  46.5 1.9 %copy.17 = f32[8,16384]{1,0:T(8,128)} copy(f32[8,16384]{1,0:T(8,128)} %get-tuple-element.4) | data formatting | bytes 1048576
  48.4 0.0 copy-done
  48.4 0.8 %copy.18 = f32[8,16384]{1,0:T(8,128)} copy(f32[8,16384]{1,0:T(8,128)S(1)} %copy-done) | data formatting | bytes 1048576
Async XLA Ops:
  46.4 1.9 %copy-start = (f32[8,16384]{1,0:T(8,128)S(1)}, f32[8,16384]{1,0:T(8,128)}, u32[]{:S(2)}) copy-start(f32[8,16384]{1,0:T(8,128)} %get-tuple-element.5) | copy-start | bytes 1572868
